TPU v7x, 512 devices: a whole 4x4x16 slice. The times are simulated.
512 devices in a mesh: dp: 8 (over y_hi, x), cls: 64 (over z, y_lo, core).
Axes of the slice: x: 4, y: 4 (y_hi: 2, y_lo: 2; y = y_hi * 2 + y_lo), z: 16, core: 2. Of those that a mesh axis runs over, the one named last changes fastest.
Arguments:
- embeddings: bfloat16 [8192, 512], P(('dp', 'cls')), may hold values from -60 to 60
- labels: int32 [8192], P('dp'), may hold values from 0 to 131071, as said below
- row_weight: float32 [8192], P('dp'), may hold values from 0.5 to 5
- prototypes: bfloat16 [131072, 512], P('cls'), may hold values from -18 to 18
Outputs:
- emb_grad: bfloat16 [8192, 512], P(('dp', 'cls'))
- proto_grad: bfloat16 [131072, 512], P('cls')
Inputs may be any that keep to these rules, and one draw needn't show every extreme that they name: `labels`: a class label of the bank for each row.
All inputs are finite; a program needn't handle non-finite values.
Results may differ from a plain program's by a relative error of at most 0.015.
Values may be sent and summed in bfloat16 or wider, within the bound.
A program may use at most 64 MiB of HBM per device.

v0:
```python
import math

import jax
import jax.numpy as jnp
from jax import lax
from jax.sharding import PartitionSpec as P

scale_factor = 64.0
margin = 0.5
sine_floor = 0.04
norm_eps = 1e-06


def unit_rows(values):
    wide = values.astype(jnp.float32)
    inverse = lax.rsqrt(jnp.sum(wide * wide, axis=1, keepdims=True) + norm_eps)
    return (inverse, wide * inverse)


def finish_rows(direction, unit_part, inverse):
    return (
        inverse * (direction - unit_part * jnp.sum(unit_part * direction, axis=1, keepdims=True))
    ).astype(jnp.bfloat16)


def total_rows(partials):
    return lax.psum(partials, "cls")


def on_device(embeddings, labels, row_weight, prototypes):
    emb_inv, emb_unit = unit_rows(embeddings)
    proto_inv, proto_unit = unit_rows(prototypes)
    unit_proto = proto_unit.astype(jnp.bfloat16)
    gathered = lax.all_gather(emb_unit.astype(jnp.bfloat16), "cls", axis=0, tiled=True)
    group_rows = gathered.shape[0]
    local_classes = prototypes.shape[0]
    block_size = min(512, group_rows)
    blocks = group_rows // block_size
    first_class = lax.axis_index("cls") * local_classes
    local_labels = labels - first_class
    emb_blocks = gathered.reshape(blocks, block_size, gathered.shape[1])
    label_blocks = local_labels.reshape(blocks, block_size)
    weight_blocks = row_weight.reshape(blocks, block_size)
    class_ids = lax.broadcasted_iota(jnp.int32, (block_size, local_classes), 1)

    def cosines(rows_bf):
        return lax.dot_general(
            rows_bf, unit_proto, (((1,), (1,)), ((), ())), preferred_element_type=jnp.float32
        )

    def margin_parts(cosine, block_labels):
        is_target = class_ids == block_labels[:, None]
        target_cos = jnp.sum(jnp.where(is_target, cosine, 0.0), axis=1)
        sine = jnp.sqrt(jnp.maximum(1.0 - target_cos * target_cos, sine_floor))
        target_logit = scale_factor * (target_cos * math.cos(margin) - sine * math.sin(margin))
        logits = jnp.where(is_target, target_logit[:, None], scale_factor * cosine)
        return (is_target, target_cos, sine, jnp.exp(logits))

    def block_grad(cosine, block_labels, block_weights, block_totals):
        is_target, target_cos, sine, exponent = margin_parts(cosine, block_labels)
        probability = exponent / block_totals[:, None]
        logit_grad = block_weights[:, None] * (probability - is_target.astype(jnp.float32))
        bound_free = 1.0 - target_cos * target_cos > sine_floor
        target_slope = scale_factor * (
            math.cos(margin) + jnp.where(bound_free, math.sin(margin) * target_cos / sine, 0.0)
        )
        slope_factor = jnp.where(is_target, target_slope[:, None], scale_factor)
        return (logit_grad * slope_factor).astype(jnp.bfloat16)

    def first_pass(pieces):
        rows_bf, block_labels = pieces
        cosine = cosines(rows_bf)
        exponent = margin_parts(cosine, block_labels)[3]
        return (cosine, jnp.sum(exponent, axis=1))

    stored, partials = lax.map(first_pass, (emb_blocks, label_blocks))
    totals = total_rows(partials.reshape(group_rows))

    def second_pass(pieces):
        cosine, block_labels, block_weights, block_totals = pieces
        return block_grad(cosine, block_labels, block_weights, block_totals)

    grad_blocks = lax.map(
        second_pass, (stored, label_blocks, weight_blocks, totals.reshape(blocks, block_size))
    )
    grad_all = grad_blocks.reshape(group_rows, local_classes)
    emb_dir = lax.psum_scatter(
        jnp.dot(grad_all, unit_proto, preferred_element_type=jnp.float32),
        "cls",
        scatter_dimension=0,
        tiled=True,
    )
    emb_grad = finish_rows(emb_dir, emb_unit, emb_inv)
    proto_part = lax.dot_general(
        grad_all, gathered, (((0,), (0,)), ((), ())), preferred_element_type=jnp.float32
    )
    proto_dir = lax.psum(proto_part.astype(jnp.bfloat16), "dp").astype(jnp.float32)
    proto_grad = finish_rows(proto_dir, proto_unit, proto_inv)
    return (emb_grad, proto_grad)


def solution(mesh):
    return jax.shard_map(
        on_device,
        mesh=mesh,
        in_specs=(P(("dp", "cls"), None), P("dp"), P("dp"), P("cls", None)),
        out_specs=(P(("dp", "cls"), None), P("cls", None)),
        check_vma=False,
    )
```

profile of v0, /device:TPU:2, one launch (start us, length us, event | category | flops | bytes accessed | tf_op | source)
XLA Modules:
  0.0 619.6 jit_solution(7776725290765595734)
XLA Ops:
  7.2 0.0 all-gather.2.cloned.1.call-start
  7.2 0.8 fusion.37
  8.1 1.4 fusion.32
  9.5 0.0 all-gather.2.cloned.1.call-update
  9.5 0.0 all-reduce.2.cloned.1.call-start
  9.6 0.7 broadcast_subtract_fusion
  10.3 0.7 reshape.192
  11.0 2.1 fusion.26
  13.1 2.0 fusion.25
  15.1 120.7 %all-gather.2.cloned.1.call-done = bf16[1024,512]{1,0:T(8,128)(2,1)} async-done(((bf16[16,512]{1,0:T(8,128)(2,1)}), bf16[1024,512]{1,0:T(8,128)(2,1)}) %all-gather.2.cloned.1.call-update) | async-done | bytes 1048592 | tf_op jit(solution)/shard_map/all_gather | solution.py:34
  135.8 12.2 %while.25 = (s32[]{:T(128)}, f32[2,512,2048]{2,1,0:T(8,128)}, f32[2,512]{1,0:T(2,128)S(1)}, bf16[2,512,512]{2,1,0:T(8,128)(2,1)}, bf16[2048,512]{1,0:T(8,128)(2,...) while((s32[]{:T(128)}, f32[2,512,2048]{2,1,0:T(8,128)}, f32[2,512]{1,0:T(2,128)S(1)}, ...), condition=%wide.region_5.6_spmd.clone, body=%wide.region_2.5_spmd.clone.sunk | while | flops 1081084416 | bytes 19422300 | solution.py:76
  135.8 4.3 bitcast_dynamic-update-slice_fusion.2
  140.0 0.7 fusion.50
  140.7 1.1 fusion.51
  141.9 4.3 bitcast_dynamic-update-slice_fusion.2
  146.2 0.7 fusion.50
  146.9 1.1 fusion.51
  148.0 107.1 %psum.14 = f32[2,512]{1,0:T(2,128)S(1)} all-reduce(f32[2,512]{1,0:T(2,128)S(1)} %get-tuple-element.81), channel_id=1, replica_groups=mesh['dp'=8,'cls'=64] {'cls'}, use_global_device_ids=true, to_apply=%region_6.7 | all-reduce | flops 1024 | bytes 8192 | tf_op jit(solution)/shard_map/psum | solution.py:27
  255.1 15.5 %while.26 = (s32[]{:T(128)}, bf16[2,512,2048]{2,1,0:T(8,128)(2,1)}, f32[2,512]{1,0:T(2,128)S(1)}, s32[2,512]{1,0:T(2,128)S(1)}, f32[2,512,2048]{2,1,0:T(8,128)}, /*index=5*/f32[2,512]{1,0:T(2,128)S(1)}, s32[]{:T(128)}) while((s32[]{:T(128)}, bf16[2,512,2048]{2,1,0:T(8,128)(2,1)}, f32[2,512]{1,0:T(2,128)S(1)}, ...), condition=%wide.region_9.10_spmd.clone.clone, body=%wide.region_7.9_spmd.clone.clone.sunk | while | flops 13637634 | bytes 10519129 | solution.py:83
  255.2 2.9 fusion.52
  258.1 4.8 fusion.53
  262.9 2.8 fusion.52
  265.8 4.8 fusion.53
  270.6 5.9 convolution_convert_fusion
  276.5 0.0 reduce-scatter.2.cloned.1.call-start
  276.6 5.8 fusion.38
  282.4 96.0 %all-reduce.2.cloned.1.call-done = bf16[2048,512]{1,0:T(8,128)(2,1)} async-done(((bf16[2048,512]{1,0:T(8,128)(2,1)}), bf16[2048,512]{1,0:T(8,128)(2,1)}) %all-reduce.2.cloned.1.call-update) | async-done | bytes 2097168 | tf_op jit(solution)/shard_map/psum | solution.py:97
  378.4 3.5 fusion.27
  381.9 2.0 fusion.29
  384.0 226.7 %reduce-scatter.2.cloned.1.call-done = f32[16,512]{1,0:T(8,128)} async-done(((f32[1024,512]{1,0:T(8,128)}), f32[16,512]{1,0:T(8,128)}) %reduce-scatter.2.cloned.1.call-update) | async-done | bytes 32784 | tf_op jit(solution)/shard_map/reduce_scatter | solution.py:87
  610.7 0.9 fusion.33
  611.6 1.4 fusion.36
  (28 shorter events, 0.3 us)
Async XLA Ops:
  7.2 128.6 %all-gather.2.cloned.1.call-start = ((), (), s32[]{:S(2)}) async-start(), calls=%async_computation.1 | async-start | bytes 1064960 | tf_op jit(solution)/shard_map/all_gather | solution.py:34
  9.5 369.0 %all-reduce.2.cloned.1.call-start = ((), (), s32[]{:S(2)}) async-start(), calls=%async_computation.3 | async-start | bytes 4194304 | tf_op jit(solution)/shard_map/psum | solution.py:97
  255.1 15.5 %copy-start.2 = (bf16[2,512,512]{2,1,0:T(8,128)(2,1)S(1)}, bf16[2,512,512]{2,1,0:T(8,128)(2,1)}, u32[]{:S(2)}) copy-start(bf16[2,512,512]{2,1,0:T(8,128)(2,1)} %get-tuple-element.296) | copy-start | bytes 3145732
  276.5 334.1 %reduce-scatter.2.cloned.1.call-start = ((), (), s32[]{:S(2)}) async-start(), calls=%async_computation.2 | async-start | bytes 2129920 | tf_op jit(solution)/shard_map/reduce_scatter | solution.py:87
  282.4 99.5 %copy-start = (bf16[2048,512]{1,0:T(8,128)(2,1)S(1)}, bf16[2048,512]{1,0:T(8,128)(2,1)}, u32[]{:S(2)}) copy-start(bf16[2048,512]{1,0:T(8,128)(2,1)} %param.11) | copy-start | bytes 6291460
  378.4 3.5 copy-start.1
  381.9 228.7 %copy-start.3 = (bf16[16,512]{1,0:T(8,128)(2,1)S(1)}, bf16[16,512]{1,0:T(8,128)(2,1)}, u32[]{:S(2)}) copy-start(bf16[16,512]{1,0:T(8,128)(2,1)} %param.8) | copy-start | bytes 49156
Sparse Core Ops, SparseCore 0:
  10.7 124.9 all-gather.1
  276.7 101.7 all-reduce.1
  381.2 229.3 reduce-scatter.1
where the time goes:
time: 620 us
  waiting for transfers between devices  443 us (71%)
  blocking collectives  107 us (17%)
  other arithmetic  33.9 us (5%)
  matrix products  20.3 us (3%)
  between operations  13.8 us (2%)
    reduce_scatter x1, waiting for transfers between devices, on_device(): lax.psum_scatter(jnp.dot(grad_all, unit_proto, preferred_element_type=jnp...  227 us
    all_gather x1, waiting for transfers between devices, on_device(): lax.all_gather(emb_unit.astype(jnp.bfloat16), 'cls', axis=0, tiled=True)  121 us
    psum x1, blocking collectives, total_rows(): return lax.psum(partials, 'cls')  107 us
    psum x1, waiting for transfers between devices, on_device(): lax.psum(proto_part.astype(jnp.bfloat16), 'dp').astype(jnp.float32)  96 us
  transfers between devices with their start and end apart: 3, of which 3 were waited for; matrix products, arithmetic and copies ran while one was open for 3% of the time, Pallas kernels for 0%

commit v1 on v0

v1 whole, which is shorter than its diff:
```python
import math

import jax
import jax.numpy as jnp
from jax import lax
from jax.experimental import pallas as pl
from jax.experimental.pallas import tpu as pltpu
from jax.sharding import PartitionSpec as P

scale_factor = 64.0
margin = 0.5
sine_floor = 0.04
norm_eps = 1e-06
log2e = 1.4426950408889634
MESH = pl.DeviceIdType.MESH
F32 = jnp.float32
BF = jnp.bfloat16

D = 512
C = 2048
R = 1024
Q = 256
CH = 256


def unit_rows(values):
    wide = values.astype(F32)
    inverse = lax.rsqrt(jnp.sum(wide * wide, axis=1, keepdims=True) + norm_eps)
    return (inverse, wide * inverse)


def finish_rows(direction, unit_part, inverse):
    return (
        inverse * (direction - unit_part * jnp.sum(unit_part * direction, axis=1, keepdims=True))
    ).astype(BF)


def kernel(
    emb_ref, lab_ref, wgt_ref, proto_hbm,
    emb_out, out,
    proto, unit, u, e, g, part,
    tot, tot_loc, tot_z,
    ra, rb, ra2, rb2, sa, sb, ta, tb,
    ed, r1, f1, r2, f2, r3, f3, r4,
    proto_sem,
    ag_s, ag_r, tl_s, tl_r, tz_s, tz_r, rs_s, rs_r, em_s, em_r,
):
    dp = lax.axis_index("dp")
    cls = lax.axis_index("cls")
    yh, x = dp // 4, dp % 4
    z, y, c = cls // 4, (cls // 2) % 2, cls % 2
    zh, zl = z // 4, z % 4

    def at_z(k):
        return (dp, ((z + k) % 16) * 4 + y * 2 + c)

    def at_local(dy, dc):
        yy = (y + dy) % 2
        cc = (c + dc) % 2
        return (dp, z * 4 + yy * 2 + cc)

    def at_x(k):
        return (yh * 4 + (x + k) % 4, cls)

    y_peer = ((1 - yh) * 4 + x, cls)
    core_peer = at_local(0, 1)
    ylo_peer = at_local(1, 0)

    def send(src, dst, ssem, rsem, where):
        cp = pltpu.make_async_remote_copy(
            src_ref=src, dst_ref=dst, send_sem=ssem, recv_sem=rsem,
            device_id=where, device_id_type=MESH,
        )
        cp.start()
        return cp

    barrier = pltpu.get_barrier_semaphore()
    friends = [at_z(k) for k in range(1, 16)]
    friends += [core_peer, ylo_peer, at_local(1, 1)]
    friends += [at_x(1), at_x(2), at_x(3), y_peer]
    for friend in friends:
        pl.semaphore_signal(barrier, inc=1, device_id=friend, device_id_type=MESH)
    load = pltpu.make_async_copy(proto_hbm, proto, proto_sem)
    load.start()
    emb_inv, emb_unit = unit_rows(emb_ref[...])
    u[c, y, zl, pl.ds(pl.multiple_of(zh * 16, 16), 16), :] = emb_unit.astype(BF)
    pl.semaphore_wait(barrier, len(friends))

    sends = []
    own_block = u.at[c, y, zl, pl.ds(pl.multiple_of(zh * 16, 16), 16)]
    p1 = [send(own_block, own_block, ag_s.at[i], ag_r.at[i], at_z(k)) for i, k in enumerate((8, 4, 12))]

    load.wait()

    def normalize(i, carry):
        rows = pl.ds(pl.multiple_of(i * CH, CH), CH)
        unit[rows, :] = unit_rows(proto[rows, :])[1].astype(BF)
        return carry

    lax.fori_loop(0, C // CH, normalize, 0)

    for cp in p1:
        cp.wait()
    own_set = u.at[c, y, zl]
    p2 = [send(own_set, own_set, ag_s.at[3 + i], ag_r.at[3 + i], at_z(k)) for i, k in enumerate((2, 1, 15))]
    toy = [send(own_set, own_set, ag_s.at[6], ag_r.at[6], ylo_peer)]
    toc = [send(own_set, own_set, ag_s.at[10], ag_r.at[10], core_peer)]
    for i, k in enumerate((2, 1, 15)):
        p2[i].wait()
        got = u.at[c, y, (zl + 16 - k) % 4]
        toy.append(send(got, got, ag_s.at[7 + i], ag_r.at[7 + i], ylo_peer))
        toc.append(send(got, got, ag_s.at[11 + i], ag_r.at[11 + i], core_peer))

    class_iota = lax.broadcasted_iota(jnp.int32, (CH, Q), 0)
    first_class = cls * C

    def first_pass(cc, yy):
        q = cc * 2 + yy
        lanes = pl.ds(pl.multiple_of(q * Q, Q), Q)
        labels = lab_ref[:, lanes] - first_class
        rows_u = u[cc, yy].reshape(Q, D)

        def step(i, carry):
            total, target = carry
            base = pl.multiple_of(i * CH, CH)
            cosine = lax.dot_general(
                unit[pl.ds(base, CH), :], rows_u, (((1,), (1,)), ((), ())),
                preferred_element_type=F32,
            )
            is_target = class_iota == labels - base
            ex = jnp.where(is_target, 0.0, jnp.exp2(cosine * (scale_factor * log2e)))
            tc = jnp.where(is_target, cosine, 0.0)
            e[q, pl.ds(base, CH), :] = ex
            total = total + jnp.sum(ex.reshape(CH // 8, 8, Q), axis=0)
            target = target + jnp.sum(tc.reshape(CH // 8, 8, Q), axis=0)
            return (total, target)

        zero = jnp.zeros((8, Q), F32)
        total, target = lax.fori_loop(0, C // CH, step, (zero, zero))
        total = jnp.sum(total, axis=0, keepdims=True)
        target_cos = jnp.sum(target, axis=0, keepdims=True)
        here = (labels >= 0) & (labels < C)
        sine = jnp.sqrt(jnp.maximum(1.0 - target_cos * target_cos, sine_floor))
        target_logit = scale_factor * (target_cos * math.cos(margin) - sine * math.sin(margin))
        target_exp = jnp.exp(target_logit)
        tot[0, :, lanes] = total + jnp.where(here, target_exp, 0.0)
        bound_free = 1.0 - target_cos * target_cos > sine_floor
        slope = scale_factor * (
            math.cos(margin) + jnp.where(bound_free, math.sin(margin) * target_cos / sine, 0.0)
        )
        tot[1, :, lanes] = target_exp
        tot[2, :, lanes] = slope

    first_pass(c, y)
    tod = []
    for i, k in enumerate((0, 2, 1, 15)):
        toy[i].wait()
        got = u.at[c, 1 - y, (zl + 16 - k) % 4]
        tod.append(send(got, got, ag_s.at[14 + i], ag_r.at[14 + i], core_peer))
    first_pass(c, 1 - y)
    for cp in toc:
        cp.wait()
    first_pass(1 - c, y)
    for cp in tod:
        cp.wait()
    first_pass(1 - c, 1 - y)

    loc = []
    for i, (dy, dc) in enumerate(((1, 0), (0, 1), (1, 1))):
        loc.append(send(tot.at[0], tot_loc.at[i], tl_s.at[i], tl_r.at[i], at_local(dy, dc)))
    for cp in loc:
        cp.wait()
    slab = tot[0] + tot_loc[0] + tot_loc[1] + tot_loc[2]
    tot[3] = slab
    along = []
    order = (8, 7, 9, 6, 10, 5, 11, 4, 12, 3, 13, 2, 14, 1, 15)
    for k in order:
        along.append(send(tot.at[3], tot_z.at[k - 1], tz_s.at[k - 1], tz_r.at[k - 1], at_z(k)))
    for cp in along:
        cp.wait()
    totals = slab
    for k in range(15):
        totals = totals + tot_z[k]

    weight = wgt_ref[...]
    row_scale = scale_factor * weight / totals
    label_grad = weight * (tot[1] / totals - 1.0) * tot[2]
    tot[4] = row_scale
    tot[5] = label_grad

    def second_pass(base):
        base = pl.multiple_of(base, CH)
        rows = pl.ds(base, CH)
        for q in range(4):
            lanes = slice(q * Q, (q + 1) * Q)
            is_target = class_iota == lab_ref[:, lanes] - (first_class + base)
            grad = jnp.where(is_target, tot[5, :, lanes], e[q, rows, :] * tot[4, :, lanes])
            g[rows, lanes] = grad.astype(BF)
        part[rows, :] = jnp.dot(
            g[rows, :], u[...].reshape(R, D), preferred_element_type=F32
        ).astype(BF)

    H = C // 2
    other = H + (1 - yh) * 512
    mine = H + yh * 512

    def rows_of(ref, start, n):
        return ref.at[pl.ds(pl.multiple_of(start, 128), n)]

    rs = []
    plan = (("x", 2), ("y", 0), ("x", 1), ("y", 1), ("x", 3))
    for kind, k in plan:
        if kind == "x":
            base = ((x + k) % 4) * 256
            second_pass(base)
            rs.append(send(rows_of(part, base, 256), ra.at[k - 1], rs_s.at[k - 1], rs_r.at[k - 1], at_x(k)))
        else:
            base = other + k * 256
            second_pass(base)
            rs.append(send(rows_of(part, base, 256), rb.at[k], rs_s.at[3 + k], rs_r.at[3 + k], y_peer))
    second_pass(x * 256)
    second_pass(mine)
    second_pass(mine + 256)

    def emb_product(cc, yy):
        q = cc * 2 + yy
        lanes = pl.ds(pl.multiple_of(q * Q, Q), Q)
        ed[cc, yy] = lax.dot_general(
            g[:, lanes], unit[...], (((0,), (0,)), ((), ())), preferred_element_type=F32
        ).astype(BF)

    emb_product(1 - c, 0)
    emb_product(1 - c, 1)
    em1 = send(ed.at[1 - c], r1, em_s.at[0], em_r.at[0], core_peer)
    emb_product(c, 0)
    emb_product(c, 1)
    em1.wait()
    f1[...] = (ed[c].astype(F32) + r1[...].astype(F32)).astype(BF).reshape(2, 4, 64, D)
    em2 = []
    for i, k in enumerate((2, 1, 15)):
        for yy in range(2):
            at = 1 + i * 2 + yy
            em2.append(send(f1.at[yy, (zl + k) % 4], r2.at[i, yy], em_s.at[at], em_r.at[at], at_z(k)))

    for cp in rs:
        cp.wait()
    n = 128
    own_a = part[pl.ds(pl.multiple_of(x * 256, 256), 256), :].astype(F32)
    sum_a = own_a + ra[0].astype(F32) + ra[1].astype(F32) + ra[2].astype(F32)
    sa[...] = sum_a.astype(BF).reshape(2, n, D)
    rs2 = [send(sa.at[1 - yh], ra2, rs_s.at[5], rs_r.at[5], y_peer)]
    own_b = part[pl.ds(pl.multiple_of(mine, 256), 512), :].astype(F32)
    sum_b = own_b + rb[...].reshape(512, D).astype(F32)
    sb[...] = sum_b.astype(BF).reshape(4, n, D)
    for k in (2, 1, 3):
        rs2.append(send(sb.at[(x + k) % 4], rb2.at[k - 1], rs_s.at[5 + k], rs_r.at[5 + k], at_x(k)))

    for cp in em2:
        cp.wait()
    f2[...] = (
        f1[:, zl].astype(F32) + r2[0].astype(F32) + r2[1].astype(F32) + r2[2].astype(F32)
    ).astype(BF)
    em3 = []
    for i, k in enumerate((8, 4, 12)):
        to = pl.ds(pl.multiple_of(((zh + k // 4) % 4) * 16, 16), 16)
        for yy in range(2):
            at = 7 + i * 2 + yy
            em3.append(send(f2.at[yy, to], r3.at[i, yy], em_s.at[at], em_r.at[at], at_z(k)))

    for cp in rs2:
        cp.wait()
    at_a = pl.multiple_of(x * 256 + yh * n, n)
    at_b = pl.multiple_of(mine + x * n, n)
    inv_a, unit_a = unit_rows(proto[pl.ds(at_a, n), :])
    dir_a = sa[yh].astype(F32) + ra2[...].astype(F32)
    out[pl.ds(at_a, n), :] = finish_rows(dir_a, unit_a, inv_a)
    ag2 = []
    mine_a = out.at[pl.ds(at_a, n)]
    ag_y = send(mine_a, mine_a, rs_s.at[9], rs_r.at[9], y_peer)
    inv_b, unit_b = unit_rows(proto[pl.ds(at_b, n), :])
    dir_b = sb[x].astype(F32) + rb2[0].astype(F32) + rb2[1].astype(F32) + rb2[2].astype(F32)
    out[pl.ds(at_b, n), :] = finish_rows(dir_b, unit_b, inv_b)
    mine_b = out.at[pl.ds(at_b, n)]
    ag_x = []
    for k in (2, 1, 3):
        ag_x.append(send(mine_b, mine_b, rs_s.at[9 + k], rs_r.at[9 + k], at_x(k)))
    ag2.append(send(mine_b, mine_b, rs_s.at[13], rs_r.at[13], y_peer))
    for k in (2, 1, 3):
        ag2.append(send(mine_a, mine_a, rs_s.at[13 + k], rs_r.at[13 + k], at_x(k)))

    for cp in em3:
        cp.wait()
    own3 = pl.ds(pl.multiple_of(zh * 16, 16), 16)
    f3[...] = (
        f2[:, own3].astype(F32) + r3[0].astype(F32) + r3[1].astype(F32) + r3[2].astype(F32)
    ).astype(BF)
    em4 = send(f3.at[1 - y], r4, em_s.at[13], em_r.at[13], ylo_peer)

    ag_y.wait()
    got = out.at[pl.ds(pl.multiple_of(x * 256 + (1 - yh) * n, n), n)]
    for k in (2, 1, 3):
        ag2.append(send(got, got, rs_s.at[16 + k], rs_r.at[16 + k], at_x(k)))
    for i, k in enumerate((2, 1, 3)):
        ag_x[i].wait()
        got = out.at[pl.ds(pl.multiple_of(mine + ((x + 4 - k) % 4) * n, n), n)]
        ag2.append(send(got, got, rs_s.at[20 + i], rs_r.at[20 + i], y_peer))

    em4.wait()
    emb_dir = f3[y].astype(F32) + r4[...].astype(F32)
    emb_inv, emb_unit = unit_rows(emb_ref[...])
    emb_out[...] = finish_rows(emb_dir, emb_unit, emb_inv)

    for cp in ag2:
        cp.wait()


def on_device(embeddings, labels, row_weight, prototypes):
    def order(values):
        return values.reshape(4, 4, 2, 2, 16).transpose(3, 2, 1, 0, 4).reshape(1, R)

    vmem = pl.BlockSpec(memory_space=pltpu.VMEM)
    dma = pltpu.SemaphoreType.DMA
    return pl.pallas_call(
        kernel,
        out_shape=(
            jax.ShapeDtypeStruct((16, D), BF),
            jax.ShapeDtypeStruct((C, D), BF),
        ),
        in_specs=[vmem, vmem, vmem, pl.BlockSpec(memory_space=pl.ANY)],
        out_specs=(vmem, vmem),
        scratch_shapes=[
            pltpu.VMEM((C, D), BF),
            pltpu.VMEM((C, D), BF),
            pltpu.VMEM((2, 2, 4, 64, D), BF),
            pltpu.VMEM((4, C, Q), F32),
            pltpu.VMEM((C, R), BF),
            pltpu.VMEM((C, D), BF),
            pltpu.VMEM((6, 1, R), F32),
            pltpu.VMEM((3, 1, R), F32),
            pltpu.VMEM((15, 1, R), F32),
            pltpu.VMEM((3, 256, D), BF),
            pltpu.VMEM((2, 256, D), BF),
            pltpu.VMEM((128, D), BF),
            pltpu.VMEM((3, 128, D), BF),
            pltpu.VMEM((2, 128, D), BF),
            pltpu.VMEM((4, 128, D), BF),
            pltpu.VMEM((128, D), BF),
            pltpu.VMEM((128, D), BF),
            pltpu.VMEM((2, 2, Q, D), BF),
            pltpu.VMEM((2, Q, D), BF),
            pltpu.VMEM((2, 4, 64, D), BF),
            pltpu.VMEM((3, 2, 64, D), BF),
            pltpu.VMEM((2, 64, D), BF),
            pltpu.VMEM((3, 2, 16, D), BF),
            pltpu.VMEM((2, 16, D), BF),
            pltpu.VMEM((16, D), BF),
            dma,
            dma((18,)), dma((18,)),
            dma((3,)), dma((3,)),
            dma((15,)), dma((15,)),
            dma((23,)), dma((23,)),
            dma((14,)), dma((14,)),
        ],
        compiler_params=pltpu.CompilerParams(
            collective_id=0, has_side_effects=True, vmem_limit_bytes=56 * 2**20
        ),
        name="margin_softmax_backward",
    )(embeddings, order(labels), order(row_weight), prototypes)


def solution(mesh):
    return jax.shard_map(
        on_device,
        mesh=mesh,
        in_specs=(P(("dp", "cls"), None), P("dp"), P("dp"), P("cls", None)),
        out_specs=(P(("dp", "cls"), None), P("cls", None)),
        check_vma=False,
    )
```

time: 620 us -> 102 us (0.16)
  the two profiles are of different devices: /device:TPU:2 before, /device:TPU:25 now
where the time goes in v1:
time: 102 us
  Pallas kernels  93.5 us (92%)
  local copies, waits for them, and re-layouts  7.34 us (7%)
    pallas_call x1, Pallas kernels, on_device(): pl.pallas_call(kernel, out_shape=(jax.ShapeDtypeStruct((16, D), BF), jax....  93.5 us
    unnamed x2, local copies, waits for them, and re-layouts  4.37 us
    reshape x4, local copies, waits for them, and re-layouts, order(): return values.reshape(4, 4, 2, 2, 16).transpose(3, 2, 1, 0, 4).reshape(1, R)  2.94 us

profile of v1, /device:TPU:25, one launch (start us, length us, event | category | flops | bytes accessed | tf_op | source)
XLA Modules:
  0.0 101.5 jit_solution(11230396842853451525)
XLA Ops:
  0.6 0.8 reshape.16
  1.4 0.7 reshape.17.lab_ref
  2.1 0.8 reshape.18
  2.9 0.7 reshape.19.wgt_ref
  3.6 93.5 %margin_softmax_backward.1 = (bf16[16,512]{1,0:T(8,128)(2,1)}, bf16[2048,512]{1,0:T(8,128)(2,1)}) custom-call(bf16[16,512]{1,0:T(8,128)(2,1)} %emb_ref.1, s32[1,1024]{1,0:T(1,128)} %reshape.17.lab_ref, f32[1,1024]{1,0:T(1,128)} %reshape.19.wgt_ref, bf16[2048,512]{1,0:T(8,128)(2,1)} %proto_hbm.1), custom_call_target="tpu_custom_call" | custom-call | tf_op jit(solution)/shard_map/margin_softmax_backward/pallas_call | solution.py:323
  97.2 1.3 %copy.10 = bf16[16,512]{1,0:T(8,128)(2,1)} copy(bf16[16,512]{1,0:T(8,128)(2,1)} %get-tuple-element.4) | data formatting | bytes 32768
  98.5 3.0 %copy.11 = bf16[2048,512]{1,0:T(8,128)(2,1)} copy(bf16[2048,512]{1,0:T(8,128)(2,1)} %get-tuple-element.5) | data formatting | bytes 4194304
  (2 shorter events, 0.0 us)

commit v2 on v1

--- a/solution.py
+++ b/solution.py
@@ -21,6 +21,7 @@
 R = 1024
 Q = 256
 CH = 256
+FH = 512
 
 
 def unit_rows(values):
@@ -35,11 +36,39 @@
     ).astype(BF)
 
 
+def order_rows(labels, weights, lab_ref, tot):
+    pieces = [(labels >> 12), (labels >> 6) & 63, labels & 63]
+    pieces = [piece.astype(F32) for piece in pieces]
+    rest = weights
+    for _ in range(3):
+        top = rest.astype(BF).astype(F32)
+        pieces.append(top)
+        rest = rest - top
+    stacked = jnp.concatenate(pieces, axis=0).astype(BF)
+    lane = lax.broadcasted_iota(jnp.int32, (128, 512), 0)
+    to = lax.broadcasted_iota(jnp.int32, (128, 512), 1)
+    from_lane = ((to >> 6) & 1) * 64 + ((to >> 7) & 1) * 32 + (to >> 8) * 16 + (to & 15)
+    move = jnp.where(lane == from_lane, 1.0, 0.0).astype(BF)
+    moved = jnp.dot(stacked, move, preferred_element_type=F32)
+    row = lax.broadcasted_iota(jnp.int32, (8, 128), 0)
+    z_high = (lax.broadcasted_iota(jnp.int32, (8, 128), 1) >> 4) & 3
+    for tile in range(8):
+        keep = row == z_high * 2 + tile % 2
+        cut = moved[:, tile // 2 * 128 : (tile // 2 + 1) * 128]
+        got = [
+            jnp.sum(jnp.where(keep, cut[8 * i : 8 * i + 8], 0.0), axis=0, keepdims=True)
+            for i in range(6)
+        ]
+        lanes = slice(tile * 128, (tile + 1) * 128)
+        lab_ref[:, lanes] = (got[0] * 4096.0 + got[1] * 64.0 + got[2]).astype(jnp.int32)
+        tot[6, :, lanes] = got[3] + got[4] + got[5]
+
+
 def kernel(
-    emb_ref, lab_ref, wgt_ref, proto_hbm,
+    emb_ref, lab_in, wgt_in, proto_hbm,
     emb_out, out,
     proto, unit, u, e, g, part,
-    tot, tot_loc, tot_z,
+    lab_ref, tot, tot_loc, tot_z,
     ra, rb, ra2, rb2, sa, sb, ta, tb,
     ed, r1, f1, r2, f2, r3, f3, r4,
     proto_sem,
@@ -97,12 +126,13 @@
         unit[rows, :] = unit_rows(proto[rows, :])[1].astype(BF)
         return carry
 
-    lax.fori_loop(0, C // CH, normalize, 0)
-
+    lax.fori_loop(0, C // CH // 2, normalize, 0)
     for cp in p1:
         cp.wait()
     own_set = u.at[c, y, zl]
     p2 = [send(own_set, own_set, ag_s.at[3 + i], ag_r.at[3 + i], at_z(k)) for i, k in enumerate((2, 1, 15))]
+    lax.fori_loop(C // CH // 2, C // CH, normalize, 0)
+    order_rows(lab_in[...], wgt_in[...], lab_ref, tot)
     toy = [send(own_set, own_set, ag_s.at[6], ag_r.at[6], ylo_peer)]
     toc = [send(own_set, own_set, ag_s.at[10], ag_r.at[10], core_peer)]
     for i, k in enumerate((2, 1, 15)):
@@ -112,6 +142,7 @@
         toc.append(send(got, got, ag_s.at[11 + i], ag_r.at[11 + i], core_peer))
 
     class_iota = lax.broadcasted_iota(jnp.int32, (CH, Q), 0)
+    wide_iota = lax.broadcasted_iota(jnp.int32, (FH, Q), 0)
     first_class = cls * C
 
     def first_pass(cc, yy):
@@ -122,21 +153,21 @@
 
         def step(i, carry):
             total, target = carry
-            base = pl.multiple_of(i * CH, CH)
+            base = pl.multiple_of(i * FH, FH)
             cosine = lax.dot_general(
-                unit[pl.ds(base, CH), :], rows_u, (((1,), (1,)), ((), ())),
+                unit[pl.ds(base, FH), :], rows_u, (((1,), (1,)), ((), ())),
                 preferred_element_type=F32,
             )
-            is_target = class_iota == labels - base
+            is_target = wide_iota == labels - base
             ex = jnp.where(is_target, 0.0, jnp.exp2(cosine * (scale_factor * log2e)))
             tc = jnp.where(is_target, cosine, 0.0)
-            e[q, pl.ds(base, CH), :] = ex
-            total = total + jnp.sum(ex.reshape(CH // 8, 8, Q), axis=0)
-            target = target + jnp.sum(tc.reshape(CH // 8, 8, Q), axis=0)
+            e[q, pl.ds(base, FH), :] = ex
+            total = total + jnp.sum(ex.reshape(FH // 8, 8, Q), axis=0)
+            target = target + jnp.sum(tc.reshape(FH // 8, 8, Q), axis=0)
             return (total, target)
 
         zero = jnp.zeros((8, Q), F32)
-        total, target = lax.fori_loop(0, C // CH, step, (zero, zero))
+        total, target = lax.fori_loop(0, C // FH, step, (zero, zero))
         total = jnp.sum(total, axis=0, keepdims=True)
         target_cos = jnp.sum(target, axis=0, keepdims=True)
         here = (labels >= 0) & (labels < C)
@@ -152,15 +183,15 @@
         tot[2, :, lanes] = slope
 
     first_pass(c, y)
+    for cp in toc:
+        cp.wait()
+    first_pass(1 - c, y)
     tod = []
     for i, k in enumerate((0, 2, 1, 15)):
         toy[i].wait()
         got = u.at[c, 1 - y, (zl + 16 - k) % 4]
         tod.append(send(got, got, ag_s.at[14 + i], ag_r.at[14 + i], core_peer))
     first_pass(c, 1 - y)
-    for cp in toc:
-        cp.wait()
-    first_pass(1 - c, y)
     for cp in tod:
         cp.wait()
     first_pass(1 - c, 1 - y)
@@ -182,7 +213,7 @@
     for k in range(15):
         totals = totals + tot_z[k]
 
-    weight = wgt_ref[...]
+    weight = tot[6]
     row_scale = scale_factor * weight / totals
     label_grad = weight * (tot[1] / totals - 1.0) * tot[2]
     tot[4] = row_scale
@@ -314,17 +345,25 @@
         cp.wait()
 
 
+def write_out(emb_grad, proto_grad, emb_out, proto_out, emb_sem, proto_sem):
+    copies = [
+        pltpu.make_async_copy(proto_grad, proto_out, proto_sem),
+        pltpu.make_async_copy(emb_grad, emb_out, emb_sem),
+    ]
+    for cp in copies:
+        cp.start()
+    for cp in copies:
+        cp.wait()
+
+
 def on_device(embeddings, labels, row_weight, prototypes):
-    def order(values):
-        return values.reshape(4, 4, 2, 2, 16).transpose(3, 2, 1, 0, 4).reshape(1, R)
-
     vmem = pl.BlockSpec(memory_space=pltpu.VMEM)
     dma = pltpu.SemaphoreType.DMA
-    return pl.pallas_call(
+    grads = pl.pallas_call(
         kernel,
         out_shape=(
-            jax.ShapeDtypeStruct((16, D), BF),
-            jax.ShapeDtypeStruct((C, D), BF),
+            pltpu.VMEM((16, D), BF),
+            pltpu.VMEM((C, D), BF),
         ),
         in_specs=[vmem, vmem, vmem, pl.BlockSpec(memory_space=pl.ANY)],
         out_specs=(vmem, vmem),
@@ -335,7 +374,8 @@
             pltpu.VMEM((4, C, Q), F32),
             pltpu.VMEM((C, R), BF),
             pltpu.VMEM((C, D), BF),
-            pltpu.VMEM((6, 1, R), F32),
+            pltpu.VMEM((1, R), jnp.int32),
+            pltpu.VMEM((7, 1, R), F32),
             pltpu.VMEM((3, 1, R), F32),
             pltpu.VMEM((15, 1, R), F32),
             pltpu.VMEM((3, 256, D), BF),
@@ -365,7 +405,19 @@
             collective_id=0, has_side_effects=True, vmem_limit_bytes=56 * 2**20
         ),
         name="margin_softmax_backward",
-    )(embeddings, order(labels), order(row_weight), prototypes)
+    )(embeddings, labels.reshape(8, 128), row_weight.reshape(8, 128), prototypes)
+    anywhere = pl.BlockSpec(memory_space=pl.ANY)
+    return pl.pallas_call(
+        write_out,
+        out_shape=(
+            jax.ShapeDtypeStruct((16, D), BF),
+            jax.ShapeDtypeStruct((C, D), BF),
+        ),
+        in_specs=[vmem, vmem],
+        out_specs=(anywhere, anywhere),
+        scratch_shapes=[dma, dma],
+        name="write_out",
+    )(*grads)
 
 
 def solution(mesh):

time: 102 us -> 94.1 us (0.923)
  the two profiles are of different devices: /device:TPU:25 before, /device:TPU:17 now
where the time goes in v2:
time: 94.1 us; the launch traced here: 93.8 us
  Pallas kernels  91.2 us (97%)
  local copies, waits for them, and re-layouts  1.93 us (2%)
    pallas_call x1, Pallas kernels, on_device(): pl.pallas_call(kernel, out_shape=(pltpu.VMEM((16, D), BF), pltpu.VMEM((C,...  88.3 us
    pallas_call x1, Pallas kernels, on_device(): pl.pallas_call(write_out, out_shape=(jax.ShapeDtypeStruct((16, D), BF), j...  2.94 us
    unnamed x4, local copies, waits for them, and re-layouts  1.93 us

profile of v2, /device:TPU:17, one launch (start us, length us, event | category | flops | bytes accessed | tf_op | source)
XLA Modules:
  0.0 93.8 jit_solution(2213397886202683617)
XLA Ops:
  0.6 88.3 %margin_softmax_backward.1 = (bf16[16,512]{1,0:T(8,128)(2,1)S(1)}, bf16[2048,512]{1,0:T(8,128)(2,1)S(1)}) custom-call(bf16[16,512]{1,0:T(8,128)(2,1)} %emb_ref.1, s32[8,128]{1,0:T(8,128)} %bitcast.2, f32[8,128]{1,0:T(8,128)} %bitcast.3, bf16[2048,512]{1,0:T(8,128)(2,1)} %proto_hbm.1), custom_call_target="tpu_custom_call" | custom-call | tf_op jit(solution)/shard_map/margin_softmax_backward/pallas_call | solution.py:362
  88.9 0.0 copy-start
  88.9 1.3 %copy-done = bf16[2048,512]{1,0:T(8,128)(2,1)} copy-done((bf16[2048,512]{1,0:T(8,128)(2,1)}, bf16[2048,512]{1,0:T(8,128)(2,1)S(1)}, u32[]{:S(2)}) %copy-start) | copy-done | bytes 2097176
  90.3 0.0 copy-start.1
  90.3 0.6 copy-done.1
  90.9 2.9 %write_out.1 = (bf16[16,512]{1,0:T(8,128)(2,1)}, bf16[2048,512]{1,0:T(8,128)(2,1)}) custom-call(bf16[16,512]{1,0:T(8,128)(2,1)} %copy-done.1, bf16[2048,512]{1,0:T(8,128)(2,1)} %copy-done), custom_call_target="tpu_custom_call" | custom-call | tf_op jit(solution)/shard_map/write_out/pallas_call | solution.py:410
Async XLA Ops:
  88.9 1.3 %copy-start = (bf16[2048,512]{1,0:T(8,128)(2,1)}, bf16[2048,512]{1,0:T(8,128)(2,1)S(1)}, u32[]{:S(2)}) copy-start(bf16[2048,512]{1,0:T(8,128)(2,1)S(1)} %get-tuple-element.5.proto_grad) | copy-start | bytes 6291460
  90.3 0.6 copy-start.1

commit v3 on v2

--- a/solution.py
+++ b/solution.py
@@ -20,6 +20,9 @@
 C = 2048
 R = 1024
 Q = 256
+NA = 144
+NB = 112
+FIRST_B = 8 * NA
 CH = 256
 FH = 512
 
@@ -69,7 +72,7 @@
     emb_out, out,
     proto, unit, u, e, g, part,
     lab_ref, tot, tot_loc, tot_z,
-    ra, rb, ra2, rb2, sa, sb, ta, tb,
+    fw, both, ra, rb, ra2, rb2, sa, sb,
     ed, r1, f1, r2, f2, r3, f3, r4,
     proto_sem,
     ag_s, ag_r, tl_s, tl_r, tz_s, tz_r, rs_s, rs_r, em_s, em_r,
@@ -141,7 +144,7 @@
         toy.append(send(got, got, ag_s.at[7 + i], ag_r.at[7 + i], ylo_peer))
         toc.append(send(got, got, ag_s.at[11 + i], ag_r.at[11 + i], core_peer))
 
-    class_iota = lax.broadcasted_iota(jnp.int32, (CH, Q), 0)
+    class_iota = lax.broadcasted_iota(jnp.int32, (2 * NA, Q), 0)
     wide_iota = lax.broadcasted_iota(jnp.int32, (FH, Q), 0)
     first_class = cls * C
 
@@ -219,39 +222,51 @@
     tot[4] = row_scale
     tot[5] = label_grad
 
-    def second_pass(base):
-        base = pl.multiple_of(base, CH)
-        rows = pl.ds(base, CH)
+    def second_pass(base, n):
+        base = pl.multiple_of(base, 16)
+        rows = pl.ds(base, n)
         for q in range(4):
             lanes = slice(q * Q, (q + 1) * Q)
-            is_target = class_iota == lab_ref[:, lanes] - (first_class + base)
+            is_target = class_iota[:n] == lab_ref[:, lanes] - (first_class + base)
             grad = jnp.where(is_target, tot[5, :, lanes], e[q, rows, :] * tot[4, :, lanes])
             g[rows, lanes] = grad.astype(BF)
         part[rows, :] = jnp.dot(
             g[rows, :], u[...].reshape(R, D), preferred_element_type=F32
         ).astype(BF)
 
-    H = C // 2
-    other = H + (1 - yh) * 512
-    mine = H + yh * 512
-
     def rows_of(ref, start, n):
-        return ref.at[pl.ds(pl.multiple_of(start, 128), n)]
-
-    rs = []
-    plan = (("x", 2), ("y", 0), ("x", 1), ("y", 1), ("x", 3))
-    for kind, k in plan:
-        if kind == "x":
-            base = ((x + k) % 4) * 256
-            second_pass(base)
-            rs.append(send(rows_of(part, base, 256), ra.at[k - 1], rs_s.at[k - 1], rs_r.at[k - 1], at_x(k)))
-        else:
-            base = other + k * 256
-            second_pass(base)
-            rs.append(send(rows_of(part, base, 256), rb.at[k], rs_s.at[3 + k], rs_r.at[3 + k], y_peer))
-    second_pass(x * 256)
-    second_pass(mine)
-    second_pass(mine + 256)
+        return ref.at[pl.ds(pl.multiple_of(start, 16), n)]
+
+    def value(ref, start, n):
+        return ref[pl.ds(pl.multiple_of(start, 16), n), :].astype(F32)
+
+    def a_rows(k):
+        return ((x + k) % 4) * (2 * NA)
+
+    other = FIRST_B + (1 - yh) * (4 * NB)
+    mine = FIRST_B + yh * (4 * NB)
+    to_left, to_right = at_x(3), at_x(1)
+
+    second_pass(a_rows(2), 2 * NA)
+    far_r = send(rows_of(part, a_rows(2), NA), fw.at[0], rs_s.at[0], rs_r.at[0], to_right)
+    far_l = send(rows_of(part, a_rows(2) + NA, NA), fw.at[1], rs_s.at[1], rs_r.at[1], to_left)
+    second_pass(other, 2 * NB)
+    rs_b = [send(rows_of(part, other, 2 * NB), rb.at[0], rs_s.at[2], rs_r.at[2], y_peer)]
+    second_pass(a_rows(1), 2 * NA)
+    rs_a = [send(rows_of(part, a_rows(1) + NA, NA), ra.at[0, 1], rs_s.at[3], rs_r.at[3], to_right)]
+    second_pass(a_rows(3), 2 * NA)
+    rs_a.append(send(rows_of(part, a_rows(3), NA), ra.at[1, 0], rs_s.at[4], rs_r.at[4], to_left))
+    second_pass(other + 2 * NB, 2 * NB)
+    rs_b.append(send(rows_of(part, other + 2 * NB, 2 * NB), rb.at[1], rs_s.at[5], rs_r.at[5], y_peer))
+    far_r.wait()
+    both[0] = (value(part, a_rows(1), NA) + fw[0].astype(F32)).astype(BF)
+    rs_a.append(send(both.at[0], ra.at[0, 0], rs_s.at[6], rs_r.at[6], to_right))
+    far_l.wait()
+    both[1] = (value(part, a_rows(3) + NA, NA) + fw[1].astype(F32)).astype(BF)
+    rs_a.append(send(both.at[1], ra.at[1, 1], rs_s.at[7], rs_r.at[7], to_left))
+    second_pass(a_rows(0), 2 * NA)
+    second_pass(mine, 2 * NB)
+    second_pass(mine + 2 * NB, 2 * NB)
 
     def emb_product(cc, yy):
         q = cc * 2 + yy
@@ -273,18 +288,20 @@
             at = 1 + i * 2 + yy
             em2.append(send(f1.at[yy, (zl + k) % 4], r2.at[i, yy], em_s.at[at], em_r.at[at], at_z(k)))
 
-    for cp in rs:
-        cp.wait()
-    n = 128
-    own_a = part[pl.ds(pl.multiple_of(x * 256, 256), 256), :].astype(F32)
-    sum_a = own_a + ra[0].astype(F32) + ra[1].astype(F32) + ra[2].astype(F32)
-    sa[...] = sum_a.astype(BF).reshape(2, n, D)
-    rs2 = [send(sa.at[1 - yh], ra2, rs_s.at[5], rs_r.at[5], y_peer)]
-    own_b = part[pl.ds(pl.multiple_of(mine, 256), 512), :].astype(F32)
-    sum_b = own_b + rb[...].reshape(512, D).astype(F32)
-    sb[...] = sum_b.astype(BF).reshape(4, n, D)
+    for cp in rs_b:
+        cp.wait()
+    sum_b = value(part, mine, 4 * NB) + rb[...].reshape(4 * NB, D).astype(F32)
+    sb[...] = sum_b.astype(BF).reshape(4, NB, D)
+    rs2 = []
     for k in (2, 1, 3):
-        rs2.append(send(sb.at[(x + k) % 4], rb2.at[k - 1], rs_s.at[5 + k], rs_r.at[5 + k], at_x(k)))
+        rs2.append(send(sb.at[(x + k) % 4], rb2.at[k - 1], rs_s.at[8 + k], rs_r.at[8 + k], at_x(k)))
+    for cp in rs_a:
+        cp.wait()
+    sum_a = value(part, a_rows(0), 2 * NA)
+    for side in range(2):
+        sum_a = sum_a + ra[side].reshape(2 * NA, D).astype(F32)
+    sa[...] = sum_a.astype(BF).reshape(2, NA, D)
+    rs2.append(send(sa.at[1 - yh], ra2, rs_s.at[8], rs_r.at[8], y_peer))
 
     for cp in em2:
         cp.wait()
@@ -300,24 +317,33 @@
 
     for cp in rs2:
         cp.wait()
-    at_a = pl.multiple_of(x * 256 + yh * n, n)
-    at_b = pl.multiple_of(mine + x * n, n)
-    inv_a, unit_a = unit_rows(proto[pl.ds(at_a, n), :])
+    serial = [12]
+
+    def pass_on(start, n, where):
+        at = serial[0]
+        serial[0] += 1
+        rows = rows_of(out, start, n)
+        return send(rows, rows, rs_s.at[at], rs_r.at[at], where)
+
+    def a_start(k, half):
+        return a_rows(k) + half * NA
+
+    def b_start(k, half):
+        return FIRST_B + half * (4 * NB) + ((x + k) % 4) * NB
+
+    mine_a, mine_b = a_start(0, yh), b_start(0, yh)
+    dir_b = value(sb.at[x], 0, NB)
+    for k in range(3):
+        dir_b = dir_b + rb2[k].astype(F32)
+    inv_b, unit_b = unit_rows(value(proto, mine_b, NB))
+    out[pl.ds(pl.multiple_of(mine_b, 16), NB), :] = finish_rows(dir_b, unit_b, inv_b)
+    b_near = [pass_on(mine_b, NB, to_right), pass_on(mine_b, NB, to_left)]
+    rest = [pass_on(mine_b, NB, y_peer)]
     dir_a = sa[yh].astype(F32) + ra2[...].astype(F32)
-    out[pl.ds(at_a, n), :] = finish_rows(dir_a, unit_a, inv_a)
-    ag2 = []
-    mine_a = out.at[pl.ds(at_a, n)]
-    ag_y = send(mine_a, mine_a, rs_s.at[9], rs_r.at[9], y_peer)
-    inv_b, unit_b = unit_rows(proto[pl.ds(at_b, n), :])
-    dir_b = sb[x].astype(F32) + rb2[0].astype(F32) + rb2[1].astype(F32) + rb2[2].astype(F32)
-    out[pl.ds(at_b, n), :] = finish_rows(dir_b, unit_b, inv_b)
-    mine_b = out.at[pl.ds(at_b, n)]
-    ag_x = []
-    for k in (2, 1, 3):
-        ag_x.append(send(mine_b, mine_b, rs_s.at[9 + k], rs_r.at[9 + k], at_x(k)))
-    ag2.append(send(mine_b, mine_b, rs_s.at[13], rs_r.at[13], y_peer))
-    for k in (2, 1, 3):
-        ag2.append(send(mine_a, mine_a, rs_s.at[13 + k], rs_r.at[13 + k], at_x(k)))
+    inv_a, unit_a = unit_rows(value(proto, mine_a, NA))
+    out[pl.ds(pl.multiple_of(mine_a, 16), NA), :] = finish_rows(dir_a, unit_a, inv_a)
+    a_cross = pass_on(mine_a, NA, y_peer)
+    a_near = [pass_on(mine_a, NA, to_right), pass_on(mine_a, NA, to_left)]
 
     for cp in em3:
         cp.wait()
@@ -327,21 +353,34 @@
     ).astype(BF)
     em4 = send(f3.at[1 - y], r4, em_s.at[13], em_r.at[13], ylo_peer)
 
-    ag_y.wait()
-    got = out.at[pl.ds(pl.multiple_of(x * 256 + (1 - yh) * n, n), n)]
-    for k in (2, 1, 3):
-        ag2.append(send(got, got, rs_s.at[16 + k], rs_r.at[16 + k], at_x(k)))
-    for i, k in enumerate((2, 1, 3)):
-        ag_x[i].wait()
-        got = out.at[pl.ds(pl.multiple_of(mine + ((x + 4 - k) % 4) * n, n), n)]
-        ag2.append(send(got, got, rs_s.at[20 + i], rs_r.at[20 + i], y_peer))
+    b_cut, a_cut = 64, 80
+    b_near[0].wait()
+    b_far = [pass_on(b_start(3, yh), b_cut, to_right)]
+    rest.append(pass_on(b_start(3, yh), NB, y_peer))
+    b_near[1].wait()
+    b_far.append(pass_on(b_start(1, yh) + b_cut, NB - b_cut, to_left))
+    rest.append(pass_on(b_start(1, yh), NB, y_peer))
+    a_cross.wait()
+    c_near = [pass_on(a_start(0, 1 - yh), NA, to_right), pass_on(a_start(0, 1 - yh), NA, to_left)]
+    a_near[0].wait()
+    rest.append(pass_on(a_start(3, yh), a_cut, to_right))
+    a_near[1].wait()
+    rest.append(pass_on(a_start(1, yh) + a_cut, NA - a_cut, to_left))
+    b_far[0].wait()
+    rest.append(pass_on(b_start(2, yh), b_cut, y_peer))
+    b_far[1].wait()
+    rest.append(pass_on(b_start(2, yh) + b_cut, NB - b_cut, y_peer))
+    c_near[0].wait()
+    rest.append(pass_on(a_start(3, 1 - yh), a_cut, to_right))
+    c_near[1].wait()
+    rest.append(pass_on(a_start(1, 1 - yh) + a_cut, NA - a_cut, to_left))
 
     em4.wait()
     emb_dir = f3[y].astype(F32) + r4[...].astype(F32)
     emb_inv, emb_unit = unit_rows(emb_ref[...])
     emb_out[...] = finish_rows(emb_dir, emb_unit, emb_inv)
 
-    for cp in ag2:
+    for cp in rest:
         cp.wait()
 
 
@@ -378,14 +417,14 @@
             pltpu.VMEM((7, 1, R), F32),
             pltpu.VMEM((3, 1, R), F32),
             pltpu.VMEM((15, 1, R), F32),
-            pltpu.VMEM((3, 256, D), BF),
-            pltpu.VMEM((2, 256, D), BF),
-            pltpu.VMEM((128, D), BF),
-            pltpu.VMEM((3, 128, D), BF),
-            pltpu.VMEM((2, 128, D), BF),
-            pltpu.VMEM((4, 128, D), BF),
-            pltpu.VMEM((128, D), BF),
-            pltpu.VMEM((128, D), BF),
+            pltpu.VMEM((2, NA, D), BF),
+            pltpu.VMEM((2, NA, D), BF),
+            pltpu.VMEM((2, 2, NA, D), BF),
+            pltpu.VMEM((2, 2 * NB, D), BF),
+            pltpu.VMEM((NA, D), BF),
+            pltpu.VMEM((3, NB, D), BF),
+            pltpu.VMEM((2, NA, D), BF),
+            pltpu.VMEM((4, NB, D), BF),
             pltpu.VMEM((2, 2, Q, D), BF),
             pltpu.VMEM((2, Q, D), BF),
             pltpu.VMEM((2, 4, 64, D), BF),
@@ -398,7 +437,7 @@
             dma((18,)), dma((18,)),
             dma((3,)), dma((3,)),
             dma((15,)), dma((15,)),
-            dma((23,)), dma((23,)),
+            dma((30,)), dma((30,)),
             dma((14,)), dma((14,)),
         ],
         compiler_params=pltpu.CompilerParams(
@@ -417,7 +456,7 @@
         out_specs=(anywhere, anywhere),
         scratch_shapes=[dma, dma],
         name="write_out",
-    )(*grads)
+    )(*[pltpu.with_memory_space_constraint(grad, pltpu.VMEM) for grad in grads])
 
 
 def solution(mesh):

time: 94.1 us -> 91.6 us (0.973)
  the two profiles are of different devices: /device:TPU:17 before, /device:TPU:32 now
where the time goes in v3:
time: 91.6 us; the launch traced here: 91.4 us
  Pallas kernels  90.8 us (99%)
    pallas_call x1, Pallas kernels, on_device(): pl.pallas_call(kernel, out_shape=(pltpu.VMEM((16, D), BF), pltpu.VMEM((C,...  89.5 us

profile of v3, /device:TPU:32, one launch (start us, length us, event | category | flops | bytes accessed | tf_op | source)
XLA Modules:
  0.0 91.4 jit_solution(14133302246228747261)
XLA Ops:
  0.6 89.5 %margin_softmax_backward.1 = (bf16[16,512]{1,0:T(8,128)(2,1)S(1)}, bf16[2048,512]{1,0:T(8,128)(2,1)S(1)}) custom-call(bf16[16,512]{1,0:T(8,128)(2,1)} %emb_ref.1, s32[8,128]{1,0:T(8,128)} %bitcast.2, f32[8,128]{1,0:T(8,128)} %bitcast.3, bf16[2048,512]{1,0:T(8,128)(2,1)} %proto_hbm.1), custom_call_target="tpu_custom_call" | custom-call | tf_op jit(solution)/shard_map/margin_softmax_backward/pallas_call | solution.py:401
  90.1 1.3 %write_out.1 = (bf16[16,512]{1,0:T(8,128)(2,1)}, bf16[2048,512]{1,0:T(8,128)(2,1)}) custom-call(bf16[16,512]{1,0:T(8,128)(2,1)S(1)} %get-tuple-element.4.emb_grad, bf16[2048,512]{1,0:T(8,128)(2,1)S(1)} %get-tuple-element.5.proto_grad), custom_call_target="tpu_custom_call" | custom-call | tf_op jit(solution)/shard_map/write_out/pallas_call | solution.py:449

commit v4 on v3

--- a/solution.py
+++ b/solution.py
@@ -24,7 +24,6 @@
 NB = 112
 FIRST_B = 8 * NA
 CH = 256
-FH = 512
 
 
 def unit_rows(values):
@@ -68,13 +67,13 @@
 
 
 def kernel(
-    emb_ref, lab_in, wgt_in, proto_hbm,
+    emb_hbm, lab_hbm, wgt_hbm, proto_hbm,
     emb_out, out,
-    proto, unit, u, e, g, part,
+    emb_ref, lab_in, wgt_in, proto, unit, u, e, g, part,
     lab_ref, tot, tot_loc, tot_z,
     fw, both, ra, rb, ra2, rb2, sa, sb,
     ed, r1, f1, r2, f2, r3, f3, r4,
-    proto_sem,
+    in_sems,
     ag_s, ag_r, tl_s, tl_r, tz_s, tz_r, rs_s, rs_r, em_s, em_r,
 ):
     dp = lax.axis_index("dp")
@@ -107,13 +106,16 @@
         return cp
 
     barrier = pltpu.get_barrier_semaphore()
-    friends = [at_z(k) for k in range(1, 16)]
+    friends = [at_z(k) for k in (8, 4, 12, 7, 9, 6, 10, 5, 11, 3, 13, 2, 14, 1, 15)]
     friends += [core_peer, ylo_peer, at_local(1, 1)]
     friends += [at_x(1), at_x(2), at_x(3), y_peer]
     for friend in friends:
         pl.semaphore_signal(barrier, inc=1, device_id=friend, device_id_type=MESH)
-    load = pltpu.make_async_copy(proto_hbm, proto, proto_sem)
-    load.start()
+    sources = ((emb_hbm, emb_ref), (lab_hbm, lab_in), (wgt_hbm, wgt_in), (proto_hbm, proto))
+    loads = [pltpu.make_async_copy(src, dst, in_sems.at[i]) for i, (src, dst) in enumerate(sources)]
+    for load in loads:
+        load.start()
+    loads[0].wait()
     emb_inv, emb_unit = unit_rows(emb_ref[...])
     u[c, y, zl, pl.ds(pl.multiple_of(zh * 16, 16), 16), :] = emb_unit.astype(BF)
     pl.semaphore_wait(barrier, len(friends))
@@ -122,7 +124,8 @@
     own_block = u.at[c, y, zl, pl.ds(pl.multiple_of(zh * 16, 16), 16)]
     p1 = [send(own_block, own_block, ag_s.at[i], ag_r.at[i], at_z(k)) for i, k in enumerate((8, 4, 12))]
 
-    load.wait()
+    for load in loads[1:]:
+        load.wait()
 
     def normalize(i, carry):
         rows = pl.ds(pl.multiple_of(i * CH, CH), CH)
@@ -133,19 +136,18 @@
     for cp in p1:
         cp.wait()
     own_set = u.at[c, y, zl]
-    p2 = [send(own_set, own_set, ag_s.at[3 + i], ag_r.at[3 + i], at_z(k)) for i, k in enumerate((2, 1, 15))]
+    p2 = [send(own_set, own_set, ag_s.at[3 + i], ag_r.at[3 + i], at_z(k)) for i, k in enumerate((1, 15, 2))]
     lax.fori_loop(C // CH // 2, C // CH, normalize, 0)
     order_rows(lab_in[...], wgt_in[...], lab_ref, tot)
     toy = [send(own_set, own_set, ag_s.at[6], ag_r.at[6], ylo_peer)]
     toc = [send(own_set, own_set, ag_s.at[10], ag_r.at[10], core_peer)]
-    for i, k in enumerate((2, 1, 15)):
+    for i, k in enumerate((1, 15, 2)):
         p2[i].wait()
         got = u.at[c, y, (zl + 16 - k) % 4]
         toy.append(send(got, got, ag_s.at[7 + i], ag_r.at[7 + i], ylo_peer))
         toc.append(send(got, got, ag_s.at[11 + i], ag_r.at[11 + i], core_peer))
 
-    class_iota = lax.broadcasted_iota(jnp.int32, (2 * NA, Q), 0)
-    wide_iota = lax.broadcasted_iota(jnp.int32, (FH, Q), 0)
+    class_iota = lax.broadcasted_iota(jnp.int32, (C, Q), 0)
     first_class = cls * C
 
     def first_pass(cc, yy):
@@ -154,25 +156,14 @@
         labels = lab_ref[:, lanes] - first_class
         rows_u = u[cc, yy].reshape(Q, D)
 
-        def step(i, carry):
-            total, target = carry
-            base = pl.multiple_of(i * FH, FH)
-            cosine = lax.dot_general(
-                unit[pl.ds(base, FH), :], rows_u, (((1,), (1,)), ((), ())),
-                preferred_element_type=F32,
-            )
-            is_target = wide_iota == labels - base
-            ex = jnp.where(is_target, 0.0, jnp.exp2(cosine * (scale_factor * log2e)))
-            tc = jnp.where(is_target, cosine, 0.0)
-            e[q, pl.ds(base, FH), :] = ex
-            total = total + jnp.sum(ex.reshape(FH // 8, 8, Q), axis=0)
-            target = target + jnp.sum(tc.reshape(FH // 8, 8, Q), axis=0)
-            return (total, target)
-
-        zero = jnp.zeros((8, Q), F32)
-        total, target = lax.fori_loop(0, C // FH, step, (zero, zero))
-        total = jnp.sum(total, axis=0, keepdims=True)
-        target_cos = jnp.sum(target, axis=0, keepdims=True)
+        cosine = lax.dot_general(
+            unit[...], rows_u, (((1,), (1,)), ((), ())), preferred_element_type=F32
+        )
+        is_target = class_iota == labels
+        ex = jnp.where(is_target, 0.0, jnp.exp2(cosine * (scale_factor * log2e)))
+        e[q] = ex
+        total = jnp.sum(ex, axis=0, keepdims=True)
+        target_cos = jnp.sum(jnp.where(is_target, cosine, 0.0), axis=0, keepdims=True)
         here = (labels >= 0) & (labels < C)
         sine = jnp.sqrt(jnp.maximum(1.0 - target_cos * target_cos, sine_floor))
         target_logit = scale_factor * (target_cos * math.cos(margin) - sine * math.sin(margin))
@@ -190,7 +181,7 @@
         cp.wait()
     first_pass(1 - c, y)
     tod = []
-    for i, k in enumerate((0, 2, 1, 15)):
+    for i, k in enumerate((0, 1, 15, 2)):
         toy[i].wait()
         got = u.at[c, 1 - y, (zl + 16 - k) % 4]
         tod.append(send(got, got, ag_s.at[14 + i], ag_r.at[14 + i], core_peer))
@@ -258,28 +249,49 @@
     rs_a.append(send(rows_of(part, a_rows(3), NA), ra.at[1, 0], rs_s.at[4], rs_r.at[4], to_left))
     second_pass(other + 2 * NB, 2 * NB)
     rs_b.append(send(rows_of(part, other + 2 * NB, 2 * NB), rb.at[1], rs_s.at[5], rs_r.at[5], y_peer))
+    second_pass(a_rows(0), 2 * NA)
+    second_pass(mine, 2 * NB)
+    second_pass(mine + 2 * NB, 2 * NB)
+
+    def emb_product(cc, yy):
+        q = cc * 2 + yy
+        lanes = pl.ds(pl.multiple_of(q * Q, Q), Q)
+        ed[cc, yy] = lax.dot_general(
+            g[:, lanes], unit[...], (((0,), (0,)), ((), ())), preferred_element_type=F32
+        ).astype(BF)
+
+    emb_product(1 - c, 0)
+    emb_product(1 - c, 1)
+    em1 = send(ed.at[1 - c], r1, em_s.at[0], em_r.at[0], core_peer)
+
     far_r.wait()
     both[0] = (value(part, a_rows(1), NA) + fw[0].astype(F32)).astype(BF)
     rs_a.append(send(both.at[0], ra.at[0, 0], rs_s.at[6], rs_r.at[6], to_right))
     far_l.wait()
     both[1] = (value(part, a_rows(3) + NA, NA) + fw[1].astype(F32)).astype(BF)
     rs_a.append(send(both.at[1], ra.at[1, 1], rs_s.at[7], rs_r.at[7], to_left))
-    second_pass(a_rows(0), 2 * NA)
-    second_pass(mine, 2 * NB)
-    second_pass(mine + 2 * NB, 2 * NB)
-
-    def emb_product(cc, yy):
-        q = cc * 2 + yy
-        lanes = pl.ds(pl.multiple_of(q * Q, Q), Q)
-        ed[cc, yy] = lax.dot_general(
-            g[:, lanes], unit[...], (((0,), (0,)), ((), ())), preferred_element_type=F32
-        ).astype(BF)
-
-    emb_product(1 - c, 0)
-    emb_product(1 - c, 1)
-    em1 = send(ed.at[1 - c], r1, em_s.at[0], em_r.at[0], core_peer)
     emb_product(c, 0)
     emb_product(c, 1)
+
+    def to_x_owner(k):
+        slot = jnp.where(k == 0, 1, k) - 1
+        return pltpu.make_async_remote_copy(
+            src_ref=sb.at[(x + k) % 4], dst_ref=rb2.at[slot],
+            send_sem=rs_s.at[9 + slot], recv_sem=rs_r.at[9 + slot],
+            device_id=at_x(k), device_id_type=MESH,
+        )
+
+    def half_b(half):
+        rs_b[half].wait()
+        sum_b = value(part, mine + half * (2 * NB), 2 * NB) + rb[half].astype(F32)
+        sb[2 * half : 2 * half + 2] = sum_b.astype(BF).reshape(2, NB, D)
+        for place in (2 * half, 2 * half + 1):
+
+            @pl.when(x != place)
+            def _():
+                to_x_owner((place + 4 - x) % 4).start()
+
+    half_b(0)
     em1.wait()
     f1[...] = (ed[c].astype(F32) + r1[...].astype(F32)).astype(BF).reshape(2, 4, 64, D)
     em2 = []
@@ -287,21 +299,45 @@
         for yy in range(2):
             at = 1 + i * 2 + yy
             em2.append(send(f1.at[yy, (zl + k) % 4], r2.at[i, yy], em_s.at[at], em_r.at[at], at_z(k)))
-
-    for cp in rs_b:
-        cp.wait()
-    sum_b = value(part, mine, 4 * NB) + rb[...].reshape(4 * NB, D).astype(F32)
-    sb[...] = sum_b.astype(BF).reshape(4, NB, D)
-    rs2 = []
-    for k in (2, 1, 3):
-        rs2.append(send(sb.at[(x + k) % 4], rb2.at[k - 1], rs_s.at[8 + k], rs_r.at[8 + k], at_x(k)))
     for cp in rs_a:
         cp.wait()
     sum_a = value(part, a_rows(0), 2 * NA)
     for side in range(2):
         sum_a = sum_a + ra[side].reshape(2 * NA, D).astype(F32)
     sa[...] = sum_a.astype(BF).reshape(2, NA, D)
-    rs2.append(send(sa.at[1 - yh], ra2, rs_s.at[8], rs_r.at[8], y_peer))
+    rs2 = [send(sa.at[1 - yh], ra2, rs_s.at[8], rs_r.at[8], y_peer)]
+    half_b(1)
+    rs2 += [to_x_owner(k) for k in (2, 1, 3)]
+
+    serial = [12]
+
+    def pass_on(start, n, where):
+        at = serial[0]
+        serial[0] += 1
+        rows = rows_of(out, start, n)
+        return send(rows, rows, rs_s.at[at], rs_r.at[at], where)
+
+    def a_start(k, half):
+        return a_rows(k) + half * NA
+
+    def b_start(k, half):
+        return FIRST_B + half * (4 * NB) + ((x + k) % 4) * NB
+
+    mine_a, mine_b = a_start(0, yh), b_start(0, yh)
+    inv_b, unit_b = unit_rows(value(proto, mine_b, NB))
+    inv_a, unit_a = unit_rows(value(proto, mine_a, NA))
+    for cp in rs2:
+        cp.wait()
+    dir_b = value(sb.at[x], 0, NB)
+    for k in range(3):
+        dir_b = dir_b + rb2[k].astype(F32)
+    out[pl.ds(pl.multiple_of(mine_b, 16), NB), :] = finish_rows(dir_b, unit_b, inv_b)
+    b_near = [pass_on(mine_b, NB, to_right), pass_on(mine_b, NB, to_left)]
+    rest = [pass_on(mine_b, NB, y_peer)]
+    dir_a = sa[yh].astype(F32) + ra2[...].astype(F32)
+    out[pl.ds(pl.multiple_of(mine_a, 16), NA), :] = finish_rows(dir_a, unit_a, inv_a)
+    a_cross = pass_on(mine_a, NA, y_peer)
+    a_near = [pass_on(mine_a, NA, to_right), pass_on(mine_a, NA, to_left)]
 
     for cp in em2:
         cp.wait()
@@ -314,44 +350,6 @@
         for yy in range(2):
             at = 7 + i * 2 + yy
             em3.append(send(f2.at[yy, to], r3.at[i, yy], em_s.at[at], em_r.at[at], at_z(k)))
-
-    for cp in rs2:
-        cp.wait()
-    serial = [12]
-
-    def pass_on(start, n, where):
-        at = serial[0]
-        serial[0] += 1
-        rows = rows_of(out, start, n)
-        return send(rows, rows, rs_s.at[at], rs_r.at[at], where)
-
-    def a_start(k, half):
-        return a_rows(k) + half * NA
-
-    def b_start(k, half):
-        return FIRST_B + half * (4 * NB) + ((x + k) % 4) * NB
-
-    mine_a, mine_b = a_start(0, yh), b_start(0, yh)
-    dir_b = value(sb.at[x], 0, NB)
-    for k in range(3):
-        dir_b = dir_b + rb2[k].astype(F32)
-    inv_b, unit_b = unit_rows(value(proto, mine_b, NB))
-    out[pl.ds(pl.multiple_of(mine_b, 16), NB), :] = finish_rows(dir_b, unit_b, inv_b)
-    b_near = [pass_on(mine_b, NB, to_right), pass_on(mine_b, NB, to_left)]
-    rest = [pass_on(mine_b, NB, y_peer)]
-    dir_a = sa[yh].astype(F32) + ra2[...].astype(F32)
-    inv_a, unit_a = unit_rows(value(proto, mine_a, NA))
-    out[pl.ds(pl.multiple_of(mine_a, 16), NA), :] = finish_rows(dir_a, unit_a, inv_a)
-    a_cross = pass_on(mine_a, NA, y_peer)
-    a_near = [pass_on(mine_a, NA, to_right), pass_on(mine_a, NA, to_left)]
-
-    for cp in em3:
-        cp.wait()
-    own3 = pl.ds(pl.multiple_of(zh * 16, 16), 16)
-    f3[...] = (
-        f2[:, own3].astype(F32) + r3[0].astype(F32) + r3[1].astype(F32) + r3[2].astype(F32)
-    ).astype(BF)
-    em4 = send(f3.at[1 - y], r4, em_s.at[13], em_r.at[13], ylo_peer)
 
     b_cut, a_cut = 64, 80
     b_near[0].wait()
@@ -370,6 +368,13 @@
     rest.append(pass_on(b_start(2, yh), b_cut, y_peer))
     b_far[1].wait()
     rest.append(pass_on(b_start(2, yh) + b_cut, NB - b_cut, y_peer))
+    for cp in em3:
+        cp.wait()
+    own3 = pl.ds(pl.multiple_of(zh * 16, 16), 16)
+    f3[...] = (
+        f2[:, own3].astype(F32) + r3[0].astype(F32) + r3[1].astype(F32) + r3[2].astype(F32)
+    ).astype(BF)
+    em4 = send(f3.at[1 - y], r4, em_s.at[13], em_r.at[13], ylo_peer)
     c_near[0].wait()
     rest.append(pass_on(a_start(3, 1 - yh), a_cut, to_right))
     c_near[1].wait()
@@ -397,6 +402,7 @@
 
 def on_device(embeddings, labels, row_weight, prototypes):
     vmem = pl.BlockSpec(memory_space=pltpu.VMEM)
+    anywhere = pl.BlockSpec(memory_space=pl.ANY)
     dma = pltpu.SemaphoreType.DMA
     grads = pl.pallas_call(
         kernel,
@@ -404,9 +410,12 @@
             pltpu.VMEM((16, D), BF),
             pltpu.VMEM((C, D), BF),
         ),
-        in_specs=[vmem, vmem, vmem, pl.BlockSpec(memory_space=pl.ANY)],
+        in_specs=[anywhere] * 4,
         out_specs=(vmem, vmem),
         scratch_shapes=[
+            pltpu.VMEM((16, D), BF),
+            pltpu.VMEM((8, 128), jnp.int32),
+            pltpu.VMEM((8, 128), F32),
             pltpu.VMEM((C, D), BF),
             pltpu.VMEM((C, D), BF),
             pltpu.VMEM((2, 2, 4, 64, D), BF),
@@ -433,7 +442,7 @@
             pltpu.VMEM((3, 2, 16, D), BF),
             pltpu.VMEM((2, 16, D), BF),
             pltpu.VMEM((16, D), BF),
-            dma,
+            dma((4,)),
             dma((18,)), dma((18,)),
             dma((3,)), dma((3,)),
             dma((15,)), dma((15,)),
@@ -445,7 +454,6 @@
         ),
         name="margin_softmax_backward",
     )(embeddings, labels.reshape(8, 128), row_weight.reshape(8, 128), prototypes)
-    anywhere = pl.BlockSpec(memory_space=pl.ANY)
     return pl.pallas_call(
         write_out,
         out_shape=(

time: 91.6 us -> 87.1 us (0.951)
  the two profiles are of different devices: /device:TPU:32 before, /device:TPU:2 now
where the time goes in v4:
time: 87.1 us; the launch traced here: 86.9 us
  Pallas kernels  86.3 us (99%)
    pallas_call x1, Pallas kernels, on_device(): pl.pallas_call(kernel, out_shape=(pltpu.VMEM((16, D), BF), pltpu.VMEM((C,...  84.9 us

profile of v4, /device:TPU:2, one launch (start us, length us, event | category | flops | bytes accessed | tf_op | source)
XLA Modules:
  0.0 86.9 jit_solution(5999922972337545497)
XLA Ops:
  0.6 84.9 %margin_softmax_backward.1 = (bf16[16,512]{1,0:T(8,128)(2,1)S(1)}, bf16[2048,512]{1,0:T(8,128)(2,1)S(1)}) custom-call(bf16[16,512]{1,0:T(8,128)(2,1)} %emb_hbm.1, s32[8,128]{1,0:T(8,128)} %bitcast.2, f32[8,128]{1,0:T(8,128)} %bitcast.3, bf16[2048,512]{1,0:T(8,128)(2,1)} %proto_hbm.1), custom_call_target="tpu_custom_call" | custom-call | tf_op jit(solution)/shard_map/margin_softmax_backward/pallas_call | solution.py:407
  85.6 1.3 %write_out.1 = (bf16[16,512]{1,0:T(8,128)(2,1)}, bf16[2048,512]{1,0:T(8,128)(2,1)}) custom-call(bf16[16,512]{1,0:T(8,128)(2,1)S(1)} %get-tuple-element.4.emb_grad, bf16[2048,512]{1,0:T(8,128)(2,1)S(1)} %get-tuple-element.5.proto_grad), custom_call_target="tpu_custom_call" | custom-call | tf_op jit(solution)/shard_map/write_out/pallas_call | solution.py:457

commit v5 on v4

--- a/solution.py
+++ b/solution.py
@@ -73,7 +73,7 @@
     lab_ref, tot, tot_loc, tot_z,
     fw, both, ra, rb, ra2, rb2, sa, sb,
     ed, r1, f1, r2, f2, r3, f3, r4,
-    in_sems,
+    in_sems, core_sem,
     ag_s, ag_r, tl_s, tl_r, tz_s, tz_r, rs_s, rs_r, em_s, em_r,
 ):
     dp = lax.axis_index("dp")
@@ -97,20 +97,29 @@
     core_peer = at_local(0, 1)
     ylo_peer = at_local(1, 0)
 
-    def send(src, dst, ssem, rsem, where):
-        cp = pltpu.make_async_remote_copy(
+    def copy_to(src, dst, ssem, rsem, where):
+        return pltpu.make_async_remote_copy(
             src_ref=src, dst_ref=dst, send_sem=ssem, recv_sem=rsem,
             device_id=where, device_id_type=MESH,
         )
+
+    def send(*args):
+        cp = copy_to(*args)
         cp.start()
         return cp
 
     barrier = pltpu.get_barrier_semaphore()
     friends = [at_z(k) for k in (8, 4, 12, 7, 9, 6, 10, 5, 11, 3, 13, 2, 14, 1, 15)]
-    friends += [core_peer, ylo_peer, at_local(1, 1)]
-    friends += [at_x(1), at_x(2), at_x(3), y_peer]
+    friends += [ylo_peer, at_x(1), at_x(2), at_x(3), y_peer]
+    partners = [core_peer, at_local(1, 1)]
     for friend in friends:
         pl.semaphore_signal(barrier, inc=1, device_id=friend, device_id_type=MESH)
+
+    @pl.when(c == 0)
+    def _():
+        for partner in partners:
+            pl.semaphore_signal(barrier, inc=1, device_id=partner, device_id_type=MESH)
+
     sources = ((emb_hbm, emb_ref), (lab_hbm, lab_in), (wgt_hbm, wgt_in), (proto_hbm, proto))
     loads = [pltpu.make_async_copy(src, dst, in_sems.at[i]) for i, (src, dst) in enumerate(sources)]
     for load in loads:
@@ -118,7 +127,17 @@
     loads[0].wait()
     emb_inv, emb_unit = unit_rows(emb_ref[...])
     u[c, y, zl, pl.ds(pl.multiple_of(zh * 16, 16), 16), :] = emb_unit.astype(BF)
-    pl.semaphore_wait(barrier, len(friends))
+
+    @pl.when(c == 0)
+    def _():
+        pl.semaphore_wait(barrier, len(friends))
+
+    @pl.when(c == 1)
+    def _():
+        pl.semaphore_wait(barrier, len(friends) + len(partners))
+        for partner in partners:
+            pl.semaphore_signal(core_sem, inc=1, device_id=partner, device_id_type=MESH)
+
 
     sends = []
     own_block = u.at[c, y, zl, pl.ds(pl.multiple_of(zh * 16, 16), 16)]
@@ -140,12 +159,10 @@
     lax.fori_loop(C // CH // 2, C // CH, normalize, 0)
     order_rows(lab_in[...], wgt_in[...], lab_ref, tot)
     toy = [send(own_set, own_set, ag_s.at[6], ag_r.at[6], ylo_peer)]
-    toc = [send(own_set, own_set, ag_s.at[10], ag_r.at[10], core_peer)]
     for i, k in enumerate((1, 15, 2)):
         p2[i].wait()
         got = u.at[c, y, (zl + 16 - k) % 4]
         toy.append(send(got, got, ag_s.at[7 + i], ag_r.at[7 + i], ylo_peer))
-        toc.append(send(got, got, ag_s.at[11 + i], ag_r.at[11 + i], core_peer))
 
     class_iota = lax.broadcasted_iota(jnp.int32, (C, Q), 0)
     first_class = cls * C
@@ -176,19 +193,49 @@
         tot[1, :, lanes] = target_exp
         tot[2, :, lanes] = slope
 
-    first_pass(c, y)
-    for cp in toc:
-        cp.wait()
-    first_pass(1 - c, y)
+    @pl.when(c == 0)
+    def _():
+        pl.semaphore_wait(core_sem, len(partners))
+
+    toc = send(u.at[c, y], u.at[c, y], ag_s.at[10], ag_r.at[10], core_peer)
     tod = []
     for i, k in enumerate((0, 1, 15, 2)):
+        got = u.at[c, 1 - y, (zl + 16 - k) % 4]
+        tod.append(copy_to(got, got, ag_s.at[14 + i], ag_r.at[14 + i], core_peer))
+
+    def other_core_here():
+        toc.wait_recv()
+        for cp in tod:
+            cp.wait_recv()
+
+    def core_0_rows(i, carry):
+        first_pass(0, i)
+        return carry
+
+    @pl.when(c == 1)
+    def _():
+        other_core_here()
+        lax.fori_loop(0, 2, core_0_rows, 0)
+
+    for i in range(4):
         toy[i].wait()
-        got = u.at[c, 1 - y, (zl + 16 - k) % 4]
-        tod.append(send(got, got, ag_s.at[14 + i], ag_r.at[14 + i], core_peer))
-    first_pass(c, 1 - y)
-    for cp in tod:
-        cp.wait()
-    first_pass(1 - c, 1 - y)
+        tod[i].start()
+
+    @pl.when(c == 0)
+    def _():
+        lax.fori_loop(0, 2, core_0_rows, 0)
+        toc.wait_recv()
+
+    first_pass(1, y)
+
+    @pl.when(c == 0)
+    def _():
+        for cp in tod:
+            cp.wait_recv()
+
+    first_pass(1, 1 - y)
+    for cp in [toc] + tod:
+        cp.wait_send()
 
     loc = []
     for i, (dy, dc) in enumerate(((1, 0), (0, 1), (1, 1))):
@@ -442,7 +489,7 @@
             pltpu.VMEM((3, 2, 16, D), BF),
             pltpu.VMEM((2, 16, D), BF),
             pltpu.VMEM((16, D), BF),
-            dma((4,)),
+            dma((4,)), pltpu.SemaphoreType.REGULAR,
             dma((18,)), dma((18,)),
             dma((3,)), dma((3,)),
             dma((15,)), dma((15,)),

time: 87.1 us -> 89.7 us (1.030)
  Pallas kernels: 86.3 us -> 88.9 us
    pallas_call x1, Pallas kernels: 84.9 us -> 87.5 us  [on_device(): pl.pallas_call(kernel, out_shape=(pltpu.VMEM((16, D), BF), pltpu.VMEM((C,...]
where the time goes in v5:
time: 89.7 us; the launch traced here: 89.5 us
  Pallas kernels  88.9 us (99%)
    pallas_call x1, Pallas kernels, on_device(): pl.pallas_call(kernel, out_shape=(pltpu.VMEM((16, D), BF), pltpu.VMEM((C,...  87.5 us

profile of v5, /device:TPU:2, one launch (start us, length us, event | category | flops | bytes accessed | tf_op | source)
XLA Modules:
  0.0 89.5 jit_solution(13432867232975318003)
XLA Ops:
  0.6 87.5 %margin_softmax_backward.1 = (bf16[16,512]{1,0:T(8,128)(2,1)S(1)}, bf16[2048,512]{1,0:T(8,128)(2,1)S(1)}) custom-call(bf16[16,512]{1,0:T(8,128)(2,1)} %emb_hbm.1, s32[8,128]{1,0:T(8,128)} %bitcast.2, f32[8,128]{1,0:T(8,128)} %bitcast.3, bf16[2048,512]{1,0:T(8,128)(2,1)} %proto_hbm.1), custom_call_target="tpu_custom_call" | custom-call | tf_op jit(solution)/shard_map/margin_softmax_backward/pallas_call | solution.py:454
  88.2 1.3 %write_out.1 = (bf16[16,512]{1,0:T(8,128)(2,1)}, bf16[2048,512]{1,0:T(8,128)(2,1)}) custom-call(bf16[16,512]{1,0:T(8,128)(2,1)S(1)} %get-tuple-element.4.emb_grad, bf16[2048,512]{1,0:T(8,128)(2,1)S(1)} %get-tuple-element.5.proto_grad), custom_call_target="tpu_custom_call" | custom-call | tf_op jit(solution)/shard_map/write_out/pallas_call | solution.py:504

commit v6 on v4

--- a/solution.py
+++ b/solution.py
@@ -70,11 +70,11 @@
     emb_hbm, lab_hbm, wgt_hbm, proto_hbm,
     emb_out, out,
     emb_ref, lab_in, wgt_in, proto, unit, u, e, g, part,
-    lab_ref, tot, tot_loc, tot_z,
+    lab_ref, tot, tot_far, tot_near,
     fw, both, ra, rb, ra2, rb2, sa, sb,
     ed, r1, f1, r2, f2, r3, f3, r4,
     in_sems,
-    ag_s, ag_r, tl_s, tl_r, tz_s, tz_r, rs_s, rs_r, em_s, em_r,
+    ag_s, ag_r, tf_s, tf_r, tn_s, tn_r, rs_s, rs_r, em_s, em_r,
 ):
     dp = lax.axis_index("dp")
     cls = lax.axis_index("cls")
@@ -85,17 +85,18 @@
     def at_z(k):
         return (dp, ((z + k) % 16) * 4 + y * 2 + c)
 
-    def at_local(dy, dc):
+    def near(k, dy, dc):
         yy = (y + dy) % 2
         cc = (c + dc) % 2
-        return (dp, z * 4 + yy * 2 + cc)
+        return (dp, ((z + k) % 16) * 4 + yy * 2 + cc)
 
     def at_x(k):
         return (yh * 4 + (x + k) % 4, cls)
 
     y_peer = ((1 - yh) * 4 + x, cls)
-    core_peer = at_local(0, 1)
-    ylo_peer = at_local(1, 0)
+    core_peer = near(0, 0, 1)
+    ylo_peer = near(0, 1, 0)
+    places = [(k, dy, dc) for k in (2, 1, 15, 0) for dy, dc in ((1, 1), (1, 0), (0, 1), (0, 0))][:-1]
 
     def send(src, dst, ssem, rsem, where):
         cp = pltpu.make_async_remote_copy(
@@ -106,8 +107,7 @@
         return cp
 
     barrier = pltpu.get_barrier_semaphore()
-    friends = [at_z(k) for k in (8, 4, 12, 7, 9, 6, 10, 5, 11, 3, 13, 2, 14, 1, 15)]
-    friends += [core_peer, ylo_peer, at_local(1, 1)]
+    friends = [at_z(k) for k in (8, 4, 12)] + [near(*place) for place in places]
     friends += [at_x(1), at_x(2), at_x(3), y_peer]
     for friend in friends:
         pl.semaphore_signal(barrier, inc=1, device_id=friend, device_id_type=MESH)
@@ -190,22 +190,20 @@
         cp.wait()
     first_pass(1 - c, 1 - y)
 
-    loc = []
-    for i, (dy, dc) in enumerate(((1, 0), (0, 1), (1, 1))):
-        loc.append(send(tot.at[0], tot_loc.at[i], tl_s.at[i], tl_r.at[i], at_local(dy, dc)))
-    for cp in loc:
-        cp.wait()
-    slab = tot[0] + tot_loc[0] + tot_loc[1] + tot_loc[2]
-    tot[3] = slab
-    along = []
-    order = (8, 7, 9, 6, 10, 5, 11, 4, 12, 3, 13, 2, 14, 1, 15)
-    for k in order:
-        along.append(send(tot.at[3], tot_z.at[k - 1], tz_s.at[k - 1], tz_r.at[k - 1], at_z(k)))
-    for cp in along:
-        cp.wait()
-    totals = slab
-    for k in range(15):
-        totals = totals + tot_z[k]
+    apart = []
+    for i, k in enumerate((8, 4, 12)):
+        apart.append(send(tot.at[0], tot_far.at[i], tf_s.at[i], tf_r.at[i], at_z(k)))
+    for cp in apart:
+        cp.wait()
+    tot[3] = tot[0] + tot_far[0] + tot_far[1] + tot_far[2]
+    around = []
+    for i, place in enumerate(places):
+        around.append(send(tot.at[3], tot_near.at[i], tn_s.at[i], tn_r.at[i], near(*place)))
+    for cp in around:
+        cp.wait()
+    totals = tot[3]
+    for i in range(15):
+        totals = totals + tot_near[i]
 
     weight = tot[6]
     row_scale = scale_factor * weight / totals
@@ -238,11 +236,11 @@
     mine = FIRST_B + yh * (4 * NB)
     to_left, to_right = at_x(3), at_x(1)
 
+    second_pass(other, 2 * NB)
+    rs_b = [send(rows_of(part, other, 2 * NB), rb.at[0], rs_s.at[2], rs_r.at[2], y_peer)]
     second_pass(a_rows(2), 2 * NA)
     far_r = send(rows_of(part, a_rows(2), NA), fw.at[0], rs_s.at[0], rs_r.at[0], to_right)
     far_l = send(rows_of(part, a_rows(2) + NA, NA), fw.at[1], rs_s.at[1], rs_r.at[1], to_left)
-    second_pass(other, 2 * NB)
-    rs_b = [send(rows_of(part, other, 2 * NB), rb.at[0], rs_s.at[2], rs_r.at[2], y_peer)]
     second_pass(a_rows(1), 2 * NA)
     rs_a = [send(rows_of(part, a_rows(1) + NA, NA), ra.at[0, 1], rs_s.at[3], rs_r.at[3], to_right)]
     second_pass(a_rows(3), 2 * NA)
@@ -326,18 +324,19 @@
     mine_a, mine_b = a_start(0, yh), b_start(0, yh)
     inv_b, unit_b = unit_rows(value(proto, mine_b, NB))
     inv_a, unit_a = unit_rows(value(proto, mine_a, NA))
-    for cp in rs2:
+    rs2[0].wait()
+    dir_a = sa[yh].astype(F32) + ra2[...].astype(F32)
+    out[pl.ds(pl.multiple_of(mine_a, 16), NA), :] = finish_rows(dir_a, unit_a, inv_a)
+    a_cross = pass_on(mine_a, NA, y_peer)
+    for cp in rs2[1:]:
         cp.wait()
     dir_b = value(sb.at[x], 0, NB)
     for k in range(3):
         dir_b = dir_b + rb2[k].astype(F32)
     out[pl.ds(pl.multiple_of(mine_b, 16), NB), :] = finish_rows(dir_b, unit_b, inv_b)
     b_near = [pass_on(mine_b, NB, to_right), pass_on(mine_b, NB, to_left)]
+    a_near = [pass_on(mine_a, NA, to_right), pass_on(mine_a, NA, to_left)]
     rest = [pass_on(mine_b, NB, y_peer)]
-    dir_a = sa[yh].astype(F32) + ra2[...].astype(F32)
-    out[pl.ds(pl.multiple_of(mine_a, 16), NA), :] = finish_rows(dir_a, unit_a, inv_a)
-    a_cross = pass_on(mine_a, NA, y_peer)
-    a_near = [pass_on(mine_a, NA, to_right), pass_on(mine_a, NA, to_left)]
 
     for cp in em2:
         cp.wait()

time: 87.1 us -> 85.6 us (0.983)
  Pallas kernels: 86.3 us -> 84.8 us
    pallas_call x1, Pallas kernels: 84.9 us -> 83.5 us  [on_device(): pl.pallas_call(kernel, out_shape=(pltpu.VMEM((16, D), BF), pltpu.VMEM((C,...]
where the time goes in v6:
time: 85.6 us; the launch traced here: 85.5 us
  Pallas kernels  84.8 us (99%)
    pallas_call x1, Pallas kernels, on_device(): pl.pallas_call(kernel, out_shape=(pltpu.VMEM((16, D), BF), pltpu.VMEM((C,...  83.5 us

profile of v6, /device:TPU:2, one launch (start us, length us, event | category | flops | bytes accessed | tf_op | source)
XLA Modules:
  0.0 85.5 jit_solution(6717818194891148605)
XLA Ops:
  0.6 83.5 %margin_softmax_backward.1 = (bf16[16,512]{1,0:T(8,128)(2,1)S(1)}, bf16[2048,512]{1,0:T(8,128)(2,1)S(1)}) custom-call(bf16[16,512]{1,0:T(8,128)(2,1)} %emb_hbm.1, s32[8,128]{1,0:T(8,128)} %bitcast.2, f32[8,128]{1,0:T(8,128)} %bitcast.3, bf16[2048,512]{1,0:T(8,128)(2,1)} %proto_hbm.1), custom_call_target="tpu_custom_call" | custom-call | tf_op jit(solution)/shard_map/margin_softmax_backward/pallas_call | solution.py:406
  84.1 1.3 %write_out.1 = (bf16[16,512]{1,0:T(8,128)(2,1)}, bf16[2048,512]{1,0:T(8,128)(2,1)}) custom-call(bf16[16,512]{1,0:T(8,128)(2,1)S(1)} %get-tuple-element.4.emb_grad, bf16[2048,512]{1,0:T(8,128)(2,1)S(1)} %get-tuple-element.5.proto_grad), custom_call_target="tpu_custom_call" | custom-call | tf_op jit(solution)/shard_map/write_out/pallas_call | solution.py:456

commit v7 on v6

--- a/solution.py
+++ b/solution.py
@@ -21,8 +21,8 @@
 R = 1024
 Q = 256
 NA = 144
-NB = 112
-FIRST_B = 8 * NA
+NB = (64, 48)
+FIRST_B = (8 * NA, 8 * (NA + NB[0]))
 CH = 256
 
 
@@ -71,11 +71,12 @@
     emb_out, out,
     emb_ref, lab_in, wgt_in, proto, unit, u, e, g, part,
     lab_ref, tot, tot_far, tot_near,
-    fw, both, ra, rb, ra2, rb2, sa, sb,
+    fw, both, ra, ra2, sa, rb0, rb1, sb0, sb1, rx0, rx1,
     ed, r1, f1, r2, f2, r3, f3, r4,
     in_sems,
     ag_s, ag_r, tf_s, tf_r, tn_s, tn_r, rs_s, rs_r, em_s, em_r,
 ):
+    rb, sb, rx = (rb0, rb1), (sb0, sb1), (rx0, rx1)
     dp = lax.axis_index("dp")
     cls = lax.axis_index("cls")
     yh, x = dp // 4, dp % 4
@@ -232,24 +233,30 @@
     def a_rows(k):
         return ((x + k) % 4) * (2 * NA)
 
-    other = FIRST_B + (1 - yh) * (4 * NB)
-    mine = FIRST_B + yh * (4 * NB)
+    def b_rows(lot, half, k=None):
+        first = FIRST_B[lot] + half * (4 * NB[lot])
+        return first if k is None else first + ((x + k) % 4) * NB[lot]
+
     to_left, to_right = at_x(3), at_x(1)
 
-    second_pass(other, 2 * NB)
-    rs_b = [send(rows_of(part, other, 2 * NB), rb.at[0], rs_s.at[2], rs_r.at[2], y_peer)]
+    def send_b(lot):
+        n = 4 * NB[lot]
+        base = b_rows(lot, 1 - yh)
+        second_pass(base, n)
+        return send(rows_of(part, base, n), rb[lot], rs_s.at[2 + lot], rs_r.at[2 + lot], y_peer)
+
+    rs_b = [send_b(0)]
     second_pass(a_rows(2), 2 * NA)
     far_r = send(rows_of(part, a_rows(2), NA), fw.at[0], rs_s.at[0], rs_r.at[0], to_right)
     far_l = send(rows_of(part, a_rows(2) + NA, NA), fw.at[1], rs_s.at[1], rs_r.at[1], to_left)
     second_pass(a_rows(1), 2 * NA)
-    rs_a = [send(rows_of(part, a_rows(1) + NA, NA), ra.at[0, 1], rs_s.at[3], rs_r.at[3], to_right)]
+    rs_a = [send(rows_of(part, a_rows(1) + NA, NA), ra.at[0, 1], rs_s.at[4], rs_r.at[4], to_right)]
     second_pass(a_rows(3), 2 * NA)
-    rs_a.append(send(rows_of(part, a_rows(3), NA), ra.at[1, 0], rs_s.at[4], rs_r.at[4], to_left))
-    second_pass(other + 2 * NB, 2 * NB)
-    rs_b.append(send(rows_of(part, other + 2 * NB, 2 * NB), rb.at[1], rs_s.at[5], rs_r.at[5], y_peer))
+    rs_a.append(send(rows_of(part, a_rows(3), NA), ra.at[1, 0], rs_s.at[5], rs_r.at[5], to_left))
+    rs_b.append(send_b(1))
     second_pass(a_rows(0), 2 * NA)
-    second_pass(mine, 2 * NB)
-    second_pass(mine + 2 * NB, 2 * NB)
+    for lot in range(2):
+        second_pass(b_rows(lot, yh), 4 * NB[lot])
 
     def emb_product(cc, yy):
         q = cc * 2 + yy
@@ -271,25 +278,18 @@
     emb_product(c, 0)
     emb_product(c, 1)
 
-    def to_x_owner(k):
-        slot = jnp.where(k == 0, 1, k) - 1
-        return pltpu.make_async_remote_copy(
-            src_ref=sb.at[(x + k) % 4], dst_ref=rb2.at[slot],
-            send_sem=rs_s.at[9 + slot], recv_sem=rs_r.at[9 + slot],
-            device_id=at_x(k), device_id_type=MESH,
-        )
-
-    def half_b(half):
-        rs_b[half].wait()
-        sum_b = value(part, mine + half * (2 * NB), 2 * NB) + rb[half].astype(F32)
-        sb[2 * half : 2 * half + 2] = sum_b.astype(BF).reshape(2, NB, D)
-        for place in (2 * half, 2 * half + 1):
-
-            @pl.when(x != place)
-            def _():
-                to_x_owner((place + 4 - x) % 4).start()
-
-    half_b(0)
+    def own_b(lot):
+        n = NB[lot]
+        rs_b[lot].wait()
+        sum_b = value(part, b_rows(lot, yh), 4 * n) + rb[lot][...].astype(F32)
+        sb[lot][...] = sum_b.astype(BF).reshape(4, n, D)
+        sent = []
+        for k in (2, 1, 3):
+            at = 8 + 3 * lot + k
+            sent.append(send(sb[lot].at[(x + k) % 4], rx[lot].at[k - 1], rs_s.at[at], rs_r.at[at], at_x(k)))
+        return sent
+
+    rs2_b = [own_b(0)]
     em1.wait()
     f1[...] = (ed[c].astype(F32) + r1[...].astype(F32)).astype(BF).reshape(2, 4, 64, D)
     em2 = []
@@ -303,11 +303,11 @@
     for side in range(2):
         sum_a = sum_a + ra[side].reshape(2 * NA, D).astype(F32)
     sa[...] = sum_a.astype(BF).reshape(2, NA, D)
-    rs2 = [send(sa.at[1 - yh], ra2, rs_s.at[8], rs_r.at[8], y_peer)]
-    half_b(1)
-    rs2 += [to_x_owner(k) for k in (2, 1, 3)]
-
-    serial = [12]
+    rs2_a = send(sa.at[1 - yh], ra2, rs_s.at[8], rs_r.at[8], y_peer)
+    rs2_b.append(own_b(1))
+
+    serial = [15]
+    rest = []
 
     def pass_on(start, n, where):
         at = serial[0]
@@ -318,25 +318,29 @@
     def a_start(k, half):
         return a_rows(k) + half * NA
 
-    def b_start(k, half):
-        return FIRST_B + half * (4 * NB) + ((x + k) % 4) * NB
-
-    mine_a, mine_b = a_start(0, yh), b_start(0, yh)
-    inv_b, unit_b = unit_rows(value(proto, mine_b, NB))
-    inv_a, unit_a = unit_rows(value(proto, mine_a, NA))
-    rs2[0].wait()
-    dir_a = sa[yh].astype(F32) + ra2[...].astype(F32)
-    out[pl.ds(pl.multiple_of(mine_a, 16), NA), :] = finish_rows(dir_a, unit_a, inv_a)
+    def store(start, n, direction):
+        inverse, unit_part = unit_rows(value(proto, start, n))
+        out[pl.ds(pl.multiple_of(start, 16), n), :] = finish_rows(direction, unit_part, inverse)
+
+    def finish_b(lot):
+        for cp in rs2_b[lot]:
+            cp.wait()
+        direction = value(sb[lot].at[x], 0, NB[lot])
+        for k in range(3):
+            direction = direction + rx[lot][k].astype(F32)
+        start = b_rows(lot, yh, 0)
+        store(start, NB[lot], direction)
+        near_b = [pass_on(start, NB[lot], to_right), pass_on(start, NB[lot], to_left)]
+        rest.append(pass_on(start, NB[lot], y_peer))
+        return near_b
+
+    b_near = [finish_b(0)]
+    rs2_a.wait()
+    mine_a = a_start(0, yh)
+    store(mine_a, NA, sa[yh].astype(F32) + ra2[...].astype(F32))
     a_cross = pass_on(mine_a, NA, y_peer)
-    for cp in rs2[1:]:
-        cp.wait()
-    dir_b = value(sb.at[x], 0, NB)
-    for k in range(3):
-        dir_b = dir_b + rb2[k].astype(F32)
-    out[pl.ds(pl.multiple_of(mine_b, 16), NB), :] = finish_rows(dir_b, unit_b, inv_b)
-    b_near = [pass_on(mine_b, NB, to_right), pass_on(mine_b, NB, to_left)]
+    b_near.append(finish_b(1))
     a_near = [pass_on(mine_a, NA, to_right), pass_on(mine_a, NA, to_left)]
-    rest = [pass_on(mine_b, NB, y_peer)]
 
     for cp in em2:
         cp.wait()
@@ -350,23 +354,41 @@
             at = 7 + i * 2 + yy
             em3.append(send(f2.at[yy, to], r3.at[i, yy], em_s.at[at], em_r.at[at], at_z(k)))
 
-    b_cut, a_cut = 64, 80
-    b_near[0].wait()
-    b_far = [pass_on(b_start(3, yh), b_cut, to_right)]
-    rest.append(pass_on(b_start(3, yh), NB, y_peer))
-    b_near[1].wait()
-    b_far.append(pass_on(b_start(1, yh) + b_cut, NB - b_cut, to_left))
-    rest.append(pass_on(b_start(1, yh), NB, y_peer))
+    b_cut, a_cut = 32, 80
+
+    def hand_on_b(lot):
+        n = NB[lot]
+        b_near[lot][0].wait()
+        left = b_rows(lot, yh, 3)
+        far = [pass_on(left, b_cut, to_right)]
+        rest.append(pass_on(left, n, y_peer))
+        b_near[lot][1].wait()
+        right = b_rows(lot, yh, 1)
+        far.append(pass_on(right + b_cut, n - b_cut, to_left))
+        rest.append(pass_on(right, n, y_peer))
+        return far
+
+    b_far = [hand_on_b(0), hand_on_b(1)]
     a_cross.wait()
-    c_near = [pass_on(a_start(0, 1 - yh), NA, to_right), pass_on(a_start(0, 1 - yh), NA, to_left)]
+    crossed = a_start(0, 1 - yh)
+    c_near = [pass_on(crossed, a_cut, to_right), pass_on(crossed + a_cut, NA - a_cut, to_left)]
+    rest.append(pass_on(crossed + a_cut, NA - a_cut, to_right))
+    rest.append(pass_on(crossed, a_cut, to_left))
     a_near[0].wait()
     rest.append(pass_on(a_start(3, yh), a_cut, to_right))
     a_near[1].wait()
     rest.append(pass_on(a_start(1, yh) + a_cut, NA - a_cut, to_left))
-    b_far[0].wait()
-    rest.append(pass_on(b_start(2, yh), b_cut, y_peer))
-    b_far[1].wait()
-    rest.append(pass_on(b_start(2, yh) + b_cut, NB - b_cut, y_peer))
+    for lot in range(2):
+        start = b_rows(lot, yh, 2)
+        b_far[lot][0].wait()
+        rest.append(pass_on(start, b_cut, y_peer))
+        b_far[lot][1].wait()
+        rest.append(pass_on(start + b_cut, NB[lot] - b_cut, y_peer))
+    c_near[0].wait()
+    rest.append(pass_on(a_start(3, 1 - yh), a_cut, to_right))
+    c_near[1].wait()
+    rest.append(pass_on(a_start(1, 1 - yh) + a_cut, NA - a_cut, to_left))
+
     for cp in em3:
         cp.wait()
     own3 = pl.ds(pl.multiple_of(zh * 16, 16), 16)
@@ -374,11 +396,6 @@
         f2[:, own3].astype(F32) + r3[0].astype(F32) + r3[1].astype(F32) + r3[2].astype(F32)
     ).astype(BF)
     em4 = send(f3.at[1 - y], r4, em_s.at[13], em_r.at[13], ylo_peer)
-    c_near[0].wait()
-    rest.append(pass_on(a_start(3, 1 - yh), a_cut, to_right))
-    c_near[1].wait()
-    rest.append(pass_on(a_start(1, 1 - yh) + a_cut, NA - a_cut, to_left))
-
     em4.wait()
     emb_dir = f3[y].astype(F32) + r4[...].astype(F32)
     emb_inv, emb_unit = unit_rows(emb_ref[...])
@@ -428,11 +445,11 @@
             pltpu.VMEM((2, NA, D), BF),
             pltpu.VMEM((2, NA, D), BF),
             pltpu.VMEM((2, 2, NA, D), BF),
-            pltpu.VMEM((2, 2 * NB, D), BF),
             pltpu.VMEM((NA, D), BF),
-            pltpu.VMEM((3, NB, D), BF),
             pltpu.VMEM((2, NA, D), BF),
-            pltpu.VMEM((4, NB, D), BF),
+            *[pltpu.VMEM((4 * n, D), BF) for n in NB],
+            *[pltpu.VMEM((4, n, D), BF) for n in NB],
+            *[pltpu.VMEM((3, n, D), BF) for n in NB],
             pltpu.VMEM((2, 2, Q, D), BF),
             pltpu.VMEM((2, Q, D), BF),
             pltpu.VMEM((2, 4, 64, D), BF),
@@ -445,7 +462,7 @@
             dma((18,)), dma((18,)),
             dma((3,)), dma((3,)),
             dma((15,)), dma((15,)),
-            dma((30,)), dma((30,)),
+            dma((48,)), dma((48,)),
             dma((14,)), dma((14,)),
         ],
         compiler_params=pltpu.CompilerParams(

time: 85.6 us -> 83.9 us (0.980)
  the two profiles are of different devices: /device:TPU:2 before, /device:TPU:4 now
where the time goes in v7:
time: 83.9 us; the launch traced here: 83.7 us
  Pallas kernels  83.1 us (99%)
    pallas_call x1, Pallas kernels, on_device(): pl.pallas_call(kernel, out_shape=(pltpu.VMEM((16, D), BF), pltpu.VMEM((C,...  81.8 us

profile of v7, /device:TPU:4, one launch (start us, length us, event | category | flops | bytes accessed | tf_op | source)
XLA Modules:
  0.0 83.7 jit_solution(9342950647885898110)
XLA Ops:
  0.6 81.8 %margin_softmax_backward.1 = (bf16[16,512]{1,0:T(8,128)(2,1)S(1)}, bf16[2048,512]{1,0:T(8,128)(2,1)S(1)}) custom-call(bf16[16,512]{1,0:T(8,128)(2,1)} %emb_hbm.1, s32[8,128]{1,0:T(8,128)} %bitcast.2, f32[8,128]{1,0:T(8,128)} %bitcast.3, bf16[2048,512]{1,0:T(8,128)(2,1)} %proto_hbm.1), custom_call_target="tpu_custom_call" | custom-call | tf_op jit(solution)/shard_map/margin_softmax_backward/pallas_call | solution.py:423
  82.4 1.3 %write_out.1 = (bf16[16,512]{1,0:T(8,128)(2,1)}, bf16[2048,512]{1,0:T(8,128)(2,1)}) custom-call(bf16[16,512]{1,0:T(8,128)(2,1)S(1)} %get-tuple-element.4.emb_grad, bf16[2048,512]{1,0:T(8,128)(2,1)S(1)} %get-tuple-element.5.proto_grad), custom_call_target="tpu_custom_call" | custom-call | tf_op jit(solution)/shard_map/write_out/pallas_call | solution.py:473

commit v8 on v7

--- a/solution.py
+++ b/solution.py
@@ -138,14 +138,19 @@
         cp.wait()
     own_set = u.at[c, y, zl]
     p2 = [send(own_set, own_set, ag_s.at[3 + i], ag_r.at[3 + i], at_z(k)) for i, k in enumerate((1, 15, 2))]
+    toy = [send(own_set, own_set, ag_s.at[6], ag_r.at[6], ylo_peer)]
+    toc = [send(own_set, own_set, ag_s.at[10], ag_r.at[10], core_peer)]
     lax.fori_loop(C // CH // 2, C // CH, normalize, 0)
     order_rows(lab_in[...], wgt_in[...], lab_ref, tot)
-    toy = [send(own_set, own_set, ag_s.at[6], ag_r.at[6], ylo_peer)]
-    toc = [send(own_set, own_set, ag_s.at[10], ag_r.at[10], core_peer)]
+    toy[0].wait()
+    beside = u.at[c, 1 - y, zl]
+    over = send(beside, beside, ag_s.at[9], ag_r.at[9], at_z(2))
+    tod = [send(beside, beside, ag_s.at[14], ag_r.at[14], core_peer)]
     for i, k in enumerate((1, 15, 2)):
         p2[i].wait()
         got = u.at[c, y, (zl + 16 - k) % 4]
-        toy.append(send(got, got, ag_s.at[7 + i], ag_r.at[7 + i], ylo_peer))
+        if k != 2:
+            toy.append(send(got, got, ag_s.at[7 + i], ag_r.at[7 + i], ylo_peer))
         toc.append(send(got, got, ag_s.at[11 + i], ag_r.at[11 + i], core_peer))
 
     class_iota = lax.broadcasted_iota(jnp.int32, (C, Q), 0)
@@ -181,11 +186,10 @@
     for cp in toc:
         cp.wait()
     first_pass(1 - c, y)
-    tod = []
-    for i, k in enumerate((0, 1, 15, 2)):
-        toy[i].wait()
+    for i, (k, arrival) in enumerate(((1, toy[1]), (15, toy[2]), (2, over))):
+        arrival.wait()
         got = u.at[c, 1 - y, (zl + 16 - k) % 4]
-        tod.append(send(got, got, ag_s.at[14 + i], ag_r.at[14 + i], core_peer))
+        tod.append(send(got, got, ag_s.at[15 + i], ag_r.at[15 + i], core_peer))
     first_pass(c, 1 - y)
     for cp in tod:
         cp.wait()
@@ -245,10 +249,10 @@
         second_pass(base, n)
         return send(rows_of(part, base, n), rb[lot], rs_s.at[2 + lot], rs_r.at[2 + lot], y_peer)
 
-    rs_b = [send_b(0)]
     second_pass(a_rows(2), 2 * NA)
     far_r = send(rows_of(part, a_rows(2), NA), fw.at[0], rs_s.at[0], rs_r.at[0], to_right)
     far_l = send(rows_of(part, a_rows(2) + NA, NA), fw.at[1], rs_s.at[1], rs_r.at[1], to_left)
+    rs_b = [send_b(0)]
     second_pass(a_rows(1), 2 * NA)
     rs_a = [send(rows_of(part, a_rows(1) + NA, NA), ra.at[0, 1], rs_s.at[4], rs_r.at[4], to_right)]
     second_pass(a_rows(3), 2 * NA)
@@ -405,11 +409,11 @@
         cp.wait()
 
 
-def write_out(emb_grad, proto_grad, emb_out, proto_out, emb_sem, proto_sem):
-    copies = [
-        pltpu.make_async_copy(proto_grad, proto_out, proto_sem),
-        pltpu.make_async_copy(emb_grad, emb_out, emb_sem),
-    ]
+def write_out(emb_grad, proto_grad, emb_out, proto_out, sems):
+    copies = [pltpu.make_async_copy(emb_grad, emb_out, sems.at[8])]
+    for i in range(8):
+        rows = pl.ds(i * (C // 8), C // 8)
+        copies.append(pltpu.make_async_copy(proto_grad.at[rows], proto_out.at[rows], sems.at[i]))
     for cp in copies:
         cp.start()
     for cp in copies:
@@ -478,7 +482,7 @@
         ),
         in_specs=[vmem, vmem],
         out_specs=(anywhere, anywhere),
-        scratch_shapes=[dma, dma],
+        scratch_shapes=[dma((9,))],
         name="write_out",
     )(*[pltpu.with_memory_space_constraint(grad, pltpu.VMEM) for grad in grads])
 

time: 83.9 us -> 83.6 us (level)
  the two profiles are of different devices: /device:TPU:4 before, /device:TPU:32 now
where the time goes in v8:
time: 83.6 us; the launch traced here: 83.4 us
  Pallas kernels  82.7 us (99%)
    pallas_call x1, Pallas kernels, on_device(): pl.pallas_call(kernel, out_shape=(pltpu.VMEM((16, D), BF), pltpu.VMEM((C,...  81.3 us

profile of v8, /device:TPU:32, one launch (start us, length us, event | category | flops | bytes accessed | tf_op | source)
XLA Modules:
  0.0 83.4 jit_solution(11977881820164504985)
XLA Ops:
  0.6 81.3 %margin_softmax_backward.1 = (bf16[16,512]{1,0:T(8,128)(2,1)S(1)}, bf16[2048,512]{1,0:T(8,128)(2,1)S(1)}) custom-call(bf16[16,512]{1,0:T(8,128)(2,1)} %emb_hbm.1, s32[8,128]{1,0:T(8,128)} %bitcast.2, f32[8,128]{1,0:T(8,128)} %bitcast.3, bf16[2048,512]{1,0:T(8,128)(2,1)} %proto_hbm.1), custom_call_target="tpu_custom_call" | custom-call | tf_op jit(solution)/shard_map/margin_softmax_backward/pallas_call | solution.py:427
  82.0 1.4 %write_out.1 = (bf16[16,512]{1,0:T(8,128)(2,1)}, bf16[2048,512]{1,0:T(8,128)(2,1)}) custom-call(bf16[16,512]{1,0:T(8,128)(2,1)S(1)} %get-tuple-element.4.emb_grad, bf16[2048,512]{1,0:T(8,128)(2,1)S(1)} %get-tuple-element.5.proto_grad), custom_call_target="tpu_custom_call" | custom-call | tf_op jit(solution)/shard_map/write_out/pallas_call | solution.py:477

commit v9 on v7

--- a/solution.py
+++ b/solution.py
@@ -20,9 +20,10 @@
 C = 2048
 R = 1024
 Q = 256
-NA = 144
+NA = (80, 64)
 NB = (64, 48)
-FIRST_B = (8 * NA, 8 * (NA + NB[0]))
+FIRST_A = (0, 8 * NA[0])
+FIRST_B = (8 * sum(NA), 8 * (sum(NA) + NB[0]))
 CH = 256
 
 
@@ -71,11 +72,12 @@
     emb_out, out,
     emb_ref, lab_in, wgt_in, proto, unit, u, e, g, part,
     lab_ref, tot, tot_far, tot_near,
-    fw, both, ra, ra2, sa, rb0, rb1, sb0, sb1, rx0, rx1,
+    fw0, fw1, both0, both1, ra0, ra1, rc0, rc1, sa0, sa1, rb0, rb1, sb0, sb1, rx0, rx1,
     ed, r1, f1, r2, f2, r3, f3, r4,
     in_sems,
     ag_s, ag_r, tf_s, tf_r, tn_s, tn_r, rs_s, rs_r, em_s, em_r,
 ):
+    fw, both, ra, ra2, sa = (fw0, fw1), (both0, both1), (ra0, ra1), (rc0, rc1), (sa0, sa1)
     rb, sb, rx = (rb0, rb1), (sb0, sb1), (rx0, rx1)
     dp = lax.axis_index("dp")
     cls = lax.axis_index("cls")
@@ -230,8 +232,8 @@
     def value(ref, start, n):
         return ref[pl.ds(pl.multiple_of(start, 16), n), :].astype(F32)
 
-    def a_rows(k):
-        return ((x + k) % 4) * (2 * NA)
+    def a_rows(lot, k):
+        return FIRST_A[lot] + ((x + k) % 4) * (2 * NA[lot])
 
     def b_rows(lot, half, k=None):
         first = FIRST_B[lot] + half * (4 * NB[lot])
@@ -239,23 +241,49 @@
 
     to_left, to_right = at_x(3), at_x(1)
 
+    serial = [0]
+
+    def ship(src, dst, where):
+        at = serial[0]
+        serial[0] += 1
+        return send(src, dst, rs_s.at[at], rs_r.at[at], where)
+
+    far, rs_a, rs_b = [], ([], []), []
+
+    def send_far(lot):
+        n, base = NA[lot], a_rows(lot, 2)
+        second_pass(base, 2 * n)
+        to_r = ship(rows_of(part, base, n), fw[lot].at[0], to_right)
+        far.append((to_r, ship(rows_of(part, base + n, n), fw[lot].at[1], to_left)))
+
+    def send_plain(lot):
+        n, base = NA[lot], a_rows(lot, 1)
+        second_pass(base, 2 * n)
+        rs_a[lot].append(ship(rows_of(part, base + n, n), ra[lot].at[0, 1], to_right))
+        base = a_rows(lot, 3)
+        second_pass(base, 2 * n)
+        rs_a[lot].append(ship(rows_of(part, base, n), ra[lot].at[1, 0], to_left))
+
+    def send_joined(lot):
+        n = NA[lot]
+        for side, start, to in ((0, a_rows(lot, 1), to_right), (1, a_rows(lot, 3) + n, to_left)):
+            far[lot][side].wait()
+            both[lot][side] = (value(part, start, n) + fw[lot][side].astype(F32)).astype(BF)
+            rs_a[lot].append(ship(both[lot].at[side], ra[lot].at[side, side], to))
+
     def send_b(lot):
-        n = 4 * NB[lot]
-        base = b_rows(lot, 1 - yh)
+        n, base = 4 * NB[lot], b_rows(lot, 1 - yh)
         second_pass(base, n)
-        return send(rows_of(part, base, n), rb[lot], rs_s.at[2 + lot], rs_r.at[2 + lot], y_peer)
-
-    rs_b = [send_b(0)]
-    second_pass(a_rows(2), 2 * NA)
-    far_r = send(rows_of(part, a_rows(2), NA), fw.at[0], rs_s.at[0], rs_r.at[0], to_right)
-    far_l = send(rows_of(part, a_rows(2) + NA, NA), fw.at[1], rs_s.at[1], rs_r.at[1], to_left)
-    second_pass(a_rows(1), 2 * NA)
-    rs_a = [send(rows_of(part, a_rows(1) + NA, NA), ra.at[0, 1], rs_s.at[4], rs_r.at[4], to_right)]
-    second_pass(a_rows(3), 2 * NA)
-    rs_a.append(send(rows_of(part, a_rows(3), NA), ra.at[1, 0], rs_s.at[5], rs_r.at[5], to_left))
-    rs_b.append(send_b(1))
-    second_pass(a_rows(0), 2 * NA)
+        rs_b.append(ship(rows_of(part, base, n), rb[lot], y_peer))
+
+    send_far(0)
+    send_far(1)
+    send_b(0)
+    send_plain(0)
+    send_plain(1)
+    send_b(1)
     for lot in range(2):
+        second_pass(a_rows(lot, 0), 2 * NA[lot])
         second_pass(b_rows(lot, yh), 4 * NB[lot])
 
     def emb_product(cc, yy):
@@ -269,12 +297,8 @@
     emb_product(1 - c, 1)
     em1 = send(ed.at[1 - c], r1, em_s.at[0], em_r.at[0], core_peer)
 
-    far_r.wait()
-    both[0] = (value(part, a_rows(1), NA) + fw[0].astype(F32)).astype(BF)
-    rs_a.append(send(both.at[0], ra.at[0, 0], rs_s.at[6], rs_r.at[6], to_right))
-    far_l.wait()
-    both[1] = (value(part, a_rows(3) + NA, NA) + fw[1].astype(F32)).astype(BF)
-    rs_a.append(send(both.at[1], ra.at[1, 1], rs_s.at[7], rs_r.at[7], to_left))
+    send_joined(0)
+    send_joined(1)
     emb_product(c, 0)
     emb_product(c, 1)
 
@@ -285,9 +309,18 @@
         sb[lot][...] = sum_b.astype(BF).reshape(4, n, D)
         sent = []
         for k in (2, 1, 3):
-            at = 8 + 3 * lot + k
-            sent.append(send(sb[lot].at[(x + k) % 4], rx[lot].at[k - 1], rs_s.at[at], rs_r.at[at], at_x(k)))
+            sent.append(ship(sb[lot].at[(x + k) % 4], rx[lot].at[k - 1], at_x(k)))
         return sent
+
+    def own_a(lot):
+        n = NA[lot]
+        for cp in rs_a[lot]:
+            cp.wait()
+        sum_a = value(part, a_rows(lot, 0), 2 * n)
+        for side in range(2):
+            sum_a = sum_a + ra[lot][side].reshape(2 * n, D).astype(F32)
+        sa[lot][...] = sum_a.astype(BF).reshape(2, n, D)
+        return ship(sa[lot].at[1 - yh], ra2[lot], y_peer)
 
     rs2_b = [own_b(0)]
     em1.wait()
@@ -297,26 +330,17 @@
         for yy in range(2):
             at = 1 + i * 2 + yy
             em2.append(send(f1.at[yy, (zl + k) % 4], r2.at[i, yy], em_s.at[at], em_r.at[at], at_z(k)))
-    for cp in rs_a:
-        cp.wait()
-    sum_a = value(part, a_rows(0), 2 * NA)
-    for side in range(2):
-        sum_a = sum_a + ra[side].reshape(2 * NA, D).astype(F32)
-    sa[...] = sum_a.astype(BF).reshape(2, NA, D)
-    rs2_a = send(sa.at[1 - yh], ra2, rs_s.at[8], rs_r.at[8], y_peer)
+    rs2_a = [own_a(0), own_a(1)]
     rs2_b.append(own_b(1))
 
-    serial = [15]
     rest = []
 
     def pass_on(start, n, where):
-        at = serial[0]
-        serial[0] += 1
         rows = rows_of(out, start, n)
-        return send(rows, rows, rs_s.at[at], rs_r.at[at], where)
-
-    def a_start(k, half):
-        return a_rows(k) + half * NA
+        return ship(rows, rows, where)
+
+    def a_start(lot, k, half):
+        return a_rows(lot, k) + half * NA[lot]
 
     def store(start, n, direction):
         inverse, unit_part = unit_rows(value(proto, start, n))
@@ -334,13 +358,16 @@
         rest.append(pass_on(start, NB[lot], y_peer))
         return near_b
 
+    def finish_a(lot):
+        n, start = NA[lot], a_start(lot, 0, yh)
+        rs2_a[lot].wait()
+        store(start, n, sa[lot][yh].astype(F32) + ra2[lot][...].astype(F32))
+        cross = pass_on(start, n, y_peer)
+        return cross, pass_on(start, n, to_right), pass_on(start, n, to_left)
+
     b_near = [finish_b(0)]
-    rs2_a.wait()
-    mine_a = a_start(0, yh)
-    store(mine_a, NA, sa[yh].astype(F32) + ra2[...].astype(F32))
-    a_cross = pass_on(mine_a, NA, y_peer)
+    a_near = [finish_a(0), finish_a(1)]
     b_near.append(finish_b(1))
-    a_near = [pass_on(mine_a, NA, to_right), pass_on(mine_a, NA, to_left)]
 
     for cp in em2:
         cp.wait()
@@ -354,40 +381,52 @@
             at = 7 + i * 2 + yy
             em3.append(send(f2.at[yy, to], r3.at[i, yy], em_s.at[at], em_r.at[at], at_z(k)))
 
-    b_cut, a_cut = 32, 80
+    a_cut, b_cut = (48, 32), (32, 16)
 
     def hand_on_b(lot):
-        n = NB[lot]
+        n, cut = NB[lot], b_cut[lot]
         b_near[lot][0].wait()
         left = b_rows(lot, yh, 3)
-        far = [pass_on(left, b_cut, to_right)]
+        far_r = pass_on(left, cut, to_right)
         rest.append(pass_on(left, n, y_peer))
         b_near[lot][1].wait()
         right = b_rows(lot, yh, 1)
-        far.append(pass_on(right + b_cut, n - b_cut, to_left))
+        far_l = pass_on(right + cut, n - cut, to_left)
         rest.append(pass_on(right, n, y_peer))
-        return far
-
-    b_far = [hand_on_b(0), hand_on_b(1)]
-    a_cross.wait()
-    crossed = a_start(0, 1 - yh)
-    c_near = [pass_on(crossed, a_cut, to_right), pass_on(crossed + a_cut, NA - a_cut, to_left)]
-    rest.append(pass_on(crossed + a_cut, NA - a_cut, to_right))
-    rest.append(pass_on(crossed, a_cut, to_left))
-    a_near[0].wait()
-    rest.append(pass_on(a_start(3, yh), a_cut, to_right))
-    a_near[1].wait()
-    rest.append(pass_on(a_start(1, yh) + a_cut, NA - a_cut, to_left))
-    for lot in range(2):
-        start = b_rows(lot, yh, 2)
+        return far_r, far_l
+
+    def cross_b(lot):
+        n, cut, start = NB[lot], b_cut[lot], b_rows(lot, yh, 2)
         b_far[lot][0].wait()
-        rest.append(pass_on(start, b_cut, y_peer))
+        rest.append(pass_on(start, cut, y_peer))
         b_far[lot][1].wait()
-        rest.append(pass_on(start + b_cut, NB[lot] - b_cut, y_peer))
-    c_near[0].wait()
-    rest.append(pass_on(a_start(3, 1 - yh), a_cut, to_right))
-    c_near[1].wait()
-    rest.append(pass_on(a_start(1, 1 - yh) + a_cut, NA - a_cut, to_left))
+        rest.append(pass_on(start + cut, n - cut, y_peer))
+
+    def spread_a(lot):
+        n, cut, start = NA[lot], a_cut[lot], a_start(lot, 0, 1 - yh)
+        a_near[lot][0].wait()
+        pair = (pass_on(start, cut, to_right), pass_on(start + cut, n - cut, to_left))
+        rest.append(pass_on(start + cut, n - cut, to_right))
+        rest.append(pass_on(start, cut, to_left))
+        return pair
+
+    def hand_on_a(lot, half, pair):
+        n, cut = NA[lot], a_cut[lot]
+        pair[0].wait()
+        rest.append(pass_on(a_start(lot, 3, half), cut, to_right))
+        pair[1].wait()
+        rest.append(pass_on(a_start(lot, 1, half) + cut, n - cut, to_left))
+
+    b_far = [hand_on_b(0)]
+    c_near = [spread_a(0)]
+    hand_on_a(0, yh, a_near[0][1:])
+    c_near.append(spread_a(1))
+    b_far.append(hand_on_b(1))
+    hand_on_a(1, yh, a_near[1][1:])
+    cross_b(0)
+    hand_on_a(0, 1 - yh, c_near[0])
+    cross_b(1)
+    hand_on_a(1, 1 - yh, c_near[1])
 
     for cp in em3:
         cp.wait()
@@ -405,11 +444,11 @@
         cp.wait()
 
 
-def write_out(emb_grad, proto_grad, emb_out, proto_out, emb_sem, proto_sem):
-    copies = [
-        pltpu.make_async_copy(proto_grad, proto_out, proto_sem),
-        pltpu.make_async_copy(emb_grad, emb_out, emb_sem),
-    ]
+def write_out(emb_grad, proto_grad, emb_out, proto_out, sems):
+    copies = [pltpu.make_async_copy(emb_grad, emb_out, sems.at[8])]
+    for i in range(8):
+        rows = pl.ds(i * (C // 8), C // 8)
+        copies.append(pltpu.make_async_copy(proto_grad.at[rows], proto_out.at[rows], sems.at[i]))
     for cp in copies:
         cp.start()
     for cp in copies:
@@ -442,11 +481,11 @@
             pltpu.VMEM((7, 1, R), F32),
             pltpu.VMEM((3, 1, R), F32),
             pltpu.VMEM((15, 1, R), F32),
-            pltpu.VMEM((2, NA, D), BF),
-            pltpu.VMEM((2, NA, D), BF),
-            pltpu.VMEM((2, 2, NA, D), BF),
-            pltpu.VMEM((NA, D), BF),
-            pltpu.VMEM((2, NA, D), BF),
+            *[pltpu.VMEM((2, n, D), BF) for n in NA],
+            *[pltpu.VMEM((2, n, D), BF) for n in NA],
+            *[pltpu.VMEM((2, 2, n, D), BF) for n in NA],
+            *[pltpu.VMEM((n, D), BF) for n in NA],
+            *[pltpu.VMEM((2, n, D), BF) for n in NA],
             *[pltpu.VMEM((4 * n, D), BF) for n in NB],
             *[pltpu.VMEM((4, n, D), BF) for n in NB],
             *[pltpu.VMEM((3, n, D), BF) for n in NB],
@@ -462,7 +501,7 @@
             dma((18,)), dma((18,)),
             dma((3,)), dma((3,)),
             dma((15,)), dma((15,)),
-            dma((48,)), dma((48,)),
+            dma((64,)), dma((64,)),
             dma((14,)), dma((14,)),
         ],
         compiler_params=pltpu.CompilerParams(
@@ -478,7 +517,7 @@
         ),
         in_specs=[vmem, vmem],
         out_specs=(anywhere, anywhere),
-        scratch_shapes=[dma, dma],
+        scratch_shapes=[dma((9,))],
         name="write_out",
     )(*[pltpu.with_memory_space_constraint(grad, pltpu.VMEM) for grad in grads])
 

time: 83.9 us -> 83.7 us (level)
  the two profiles are of different devices: /device:TPU:4 before, /device:TPU:2 now
where the time goes in v9:
time: 83.7 us; the launch traced here: 83.5 us
  Pallas kernels  82.9 us (99%)
    pallas_call x1, Pallas kernels, on_device(): pl.pallas_call(kernel, out_shape=(pltpu.VMEM((16, D), BF), pltpu.VMEM((C,...  81.5 us

profile of v9, /device:TPU:2, one launch (start us, length us, event | category | flops | bytes accessed | tf_op | source)
XLA Modules:
  0.0 83.5 jit_solution(3996357028634004949)
XLA Ops:
  0.6 81.5 %margin_softmax_backward.1 = (bf16[16,512]{1,0:T(8,128)(2,1)S(1)}, bf16[2048,512]{1,0:T(8,128)(2,1)S(1)}) custom-call(bf16[16,512]{1,0:T(8,128)(2,1)} %emb_hbm.1, s32[8,128]{1,0:T(8,128)} %bitcast.2, f32[8,128]{1,0:T(8,128)} %bitcast.3, bf16[2048,512]{1,0:T(8,128)(2,1)} %proto_hbm.1), custom_call_target="tpu_custom_call" | custom-call | tf_op jit(solution)/shard_map/margin_softmax_backward/pallas_call | solution.py:462
  82.1 1.4 %write_out.1 = (bf16[16,512]{1,0:T(8,128)(2,1)}, bf16[2048,512]{1,0:T(8,128)(2,1)}) custom-call(bf16[16,512]{1,0:T(8,128)(2,1)S(1)} %get-tuple-element.4.emb_grad, bf16[2048,512]{1,0:T(8,128)(2,1)S(1)} %get-tuple-element.5.proto_grad), custom_call_target="tpu_custom_call" | custom-call | tf_op jit(solution)/shard_map/write_out/pallas_call | solution.py:512

commit v10 on v9

--- a/solution.py
+++ b/solution.py
@@ -334,6 +334,7 @@
     rs2_b.append(own_b(1))
 
     rest = []
+    direct_a, direct_b = (1,), (1,)
 
     def pass_on(start, n, where):
         rows = rows_of(out, start, n)
@@ -355,6 +356,8 @@
         start = b_rows(lot, yh, 0)
         store(start, NB[lot], direction)
         near_b = [pass_on(start, NB[lot], to_right), pass_on(start, NB[lot], to_left)]
+        if lot in direct_b:
+            near_b.append(pass_on(start, NB[lot], at_x(2)))
         rest.append(pass_on(start, NB[lot], y_peer))
         return near_b
 
@@ -387,16 +390,23 @@
         n, cut = NB[lot], b_cut[lot]
         b_near[lot][0].wait()
         left = b_rows(lot, yh, 3)
-        far_r = pass_on(left, cut, to_right)
+        far_r = far_l = None
+        if lot not in direct_b:
+            far_r = pass_on(left, cut, to_right)
         rest.append(pass_on(left, n, y_peer))
         b_near[lot][1].wait()
         right = b_rows(lot, yh, 1)
-        far_l = pass_on(right + cut, n - cut, to_left)
+        if lot not in direct_b:
+            far_l = pass_on(right + cut, n - cut, to_left)
         rest.append(pass_on(right, n, y_peer))
         return far_r, far_l
 
     def cross_b(lot):
         n, cut, start = NB[lot], b_cut[lot], b_rows(lot, yh, 2)
+        if lot in direct_b:
+            b_near[lot][2].wait()
+            rest.append(pass_on(start, n, y_peer))
+            return
         b_far[lot][0].wait()
         rest.append(pass_on(start, cut, y_peer))
         b_far[lot][1].wait()
@@ -405,12 +415,18 @@
     def spread_a(lot):
         n, cut, start = NA[lot], a_cut[lot], a_start(lot, 0, 1 - yh)
         a_near[lot][0].wait()
+        if lot in direct_a:
+            for k in (2, 1, 3):
+                rest.append(pass_on(start, n, at_x(k)))
+            return None
         pair = (pass_on(start, cut, to_right), pass_on(start + cut, n - cut, to_left))
         rest.append(pass_on(start + cut, n - cut, to_right))
         rest.append(pass_on(start, cut, to_left))
         return pair
 
     def hand_on_a(lot, half, pair):
+        if pair is None:
+            return
         n, cut = NA[lot], a_cut[lot]
         pair[0].wait()
         rest.append(pass_on(a_start(lot, 3, half), cut, to_right))

time: 83.7 us -> 83.1 us (level)
  the two profiles are of different devices: /device:TPU:2 before, /device:TPU:1 now
where the time goes in v10:
time: 83.1 us; the launch traced here: 82.9 us
  Pallas kernels  82.3 us (99%)
    pallas_call x1, Pallas kernels, on_device(): pl.pallas_call(kernel, out_shape=(pltpu.VMEM((16, D), BF), pltpu.VMEM((C,...  80.9 us

profile of v10, /device:TPU:1, one launch (start us, length us, event | category | flops | bytes accessed | tf_op | source)
XLA Modules:
  0.0 82.9 jit_solution(15623144149480860036)
XLA Ops:
  0.6 80.9 %margin_softmax_backward.1 = (bf16[16,512]{1,0:T(8,128)(2,1)S(1)}, bf16[2048,512]{1,0:T(8,128)(2,1)S(1)}) custom-call(bf16[16,512]{1,0:T(8,128)(2,1)} %emb_hbm.1, s32[8,128]{1,0:T(8,128)} %bitcast.2, f32[8,128]{1,0:T(8,128)} %bitcast.3, bf16[2048,512]{1,0:T(8,128)(2,1)} %proto_hbm.1), custom_call_target="tpu_custom_call" | custom-call | tf_op jit(solution)/shard_map/margin_softmax_backward/pallas_call | solution.py:478
  81.5 1.4 %write_out.1 = (bf16[16,512]{1,0:T(8,128)(2,1)}, bf16[2048,512]{1,0:T(8,128)(2,1)}) custom-call(bf16[16,512]{1,0:T(8,128)(2,1)S(1)} %get-tuple-element.4.emb_grad, bf16[2048,512]{1,0:T(8,128)(2,1)S(1)} %get-tuple-element.5.proto_grad), custom_call_target="tpu_custom_call" | custom-call | tf_op jit(solution)/shard_map/write_out/pallas_call | solution.py:528

commit v11 on v10

--- a/solution.py
+++ b/solution.py
@@ -20,7 +20,7 @@
 C = 2048
 R = 1024
 Q = 256
-NA = (80, 64)
+NA = (96, 48)
 NB = (64, 48)
 FIRST_A = (0, 8 * NA[0])
 FIRST_B = (8 * sum(NA), 8 * (sum(NA) + NB[0]))
@@ -384,7 +384,7 @@
             at = 7 + i * 2 + yy
             em3.append(send(f2.at[yy, to], r3.at[i, yy], em_s.at[at], em_r.at[at], at_z(k)))
 
-    a_cut, b_cut = (48, 32), (32, 16)
+    a_cut, b_cut = (48, 16), (32, 16)
 
     def hand_on_b(lot):
         n, cut = NB[lot], b_cut[lot]

time: 83.1 us -> 81.9 us (0.986)
  Pallas kernels: 82.3 us -> 81.1 us
    pallas_call x1, Pallas kernels: 80.9 us -> 79.7 us  [on_device(): pl.pallas_call(kernel, out_shape=(pltpu.VMEM((16, D), BF), pltpu.VMEM((C,...]
where the time goes in v11:
time: 81.9 us; the launch traced here: 81.7 us
  Pallas kernels  81.1 us (99%)
    pallas_call x1, Pallas kernels, on_device(): pl.pallas_call(kernel, out_shape=(pltpu.VMEM((16, D), BF), pltpu.VMEM((C,...  79.7 us

profile of v11, /device:TPU:1, one launch (start us, length us, event | category | flops | bytes accessed | tf_op | source)
XLA Modules:
  0.0 81.7 jit_solution(3471220012277454030)
XLA Ops:
  0.6 79.7 %margin_softmax_backward.1 = (bf16[16,512]{1,0:T(8,128)(2,1)S(1)}, bf16[2048,512]{1,0:T(8,128)(2,1)S(1)}) custom-call(bf16[16,512]{1,0:T(8,128)(2,1)} %emb_hbm.1, s32[8,128]{1,0:T(8,128)} %bitcast.2, f32[8,128]{1,0:T(8,128)} %bitcast.3, bf16[2048,512]{1,0:T(8,128)(2,1)} %proto_hbm.1), custom_call_target="tpu_custom_call" | custom-call | tf_op jit(solution)/shard_map/margin_softmax_backward/pallas_call | solution.py:478
  80.3 1.4 %write_out.1 = (bf16[16,512]{1,0:T(8,128)(2,1)}, bf16[2048,512]{1,0:T(8,128)(2,1)}) custom-call(bf16[16,512]{1,0:T(8,128)(2,1)S(1)} %get-tuple-element.4.emb_grad, bf16[2048,512]{1,0:T(8,128)(2,1)S(1)} %get-tuple-element.5.proto_grad), custom_call_target="tpu_custom_call" | custom-call | tf_op jit(solution)/shard_map/write_out/pallas_call | solution.py:528
